TPU v7x, 128 devices: a whole 4x4x4 slice. The times are simulated.
128 devices in a mesh: gx: 16 (over x, z_hi, core), gy: 4 (over y), gz: 2 (over z_lo).
Axes of the slice: x: 4, y: 4, z: 4 (z_hi: 2, z_lo: 2; z = z_hi * 2 + z_lo), core: 2. Of those that a mesh axis runs over, the one named last changes fastest.
Arguments:
- positions: float32 [3, 32, 8, 4, 128], P(None, 'gx', 'gy', 'gz'), may hold values from 0 to 1
- velocities: float32 [3, 32, 8, 4, 128], P(None, 'gx', 'gy', 'gz'), may hold values from -3 to 3
- spins: float32 [3, 32, 8, 4, 128], P(None, 'gx', 'gy', 'gz'), may hold values from -6 to 6
- radii: float32 [32, 8, 4, 128], P('gx', 'gy', 'gz'), may hold values from 0.08 to 0.13
- counts: int32 [32, 8, 4], P('gx', 'gy', 'gz'), may hold values from 16 to 128
- springs: float32 [3, 4, 32, 8, 4, 128], P(None, None, 'gx', 'gy', 'gz'), may hold values from -0.36 to 0.36
- partners: int32 [4, 32, 8, 4, 128], P(None, 'gx', 'gy', 'gz'), may hold values from -1 to 895, as said below
- cells: int32 [32, 8, 4, 128], P('gx', 'gy', 'gz'), may hold values from 0 to 16383
- departures: int32 [16, 4, 2, 6, 128], P('gx', 'gy', 'gz'), may hold values from -1 to 1023, as said below
- fluid_velocity: float32 [3, 256, 128, 512], P(None, 'gx', 'gy', 'gz'), may hold values from -6 to 6
- pressure: float32 [256, 128, 512], P('gx', 'gy', 'gz'), may hold values from -6 to 6
- pressure_source: float32 [256, 128, 512], P('gx', 'gy', 'gz'), may hold values from -6 to 6
Outputs:
- new_positions: float32 [3, 32, 8, 4, 128], P(None, 'gx', 'gy', 'gz')
- new_velocities: float32 [3, 32, 8, 4, 128], P(None, 'gx', 'gy', 'gz')
- new_spins: float32 [3, 32, 8, 4, 128], P(None, 'gx', 'gy', 'gz')
- new_springs: float32 [3, 4, 32, 8, 4, 128], P(None, None, 'gx', 'gy', 'gz')
- fluid_force: float32 [3, 256, 128, 512], P(None, 'gx', 'gy', 'gz')
- new_pressure: float32 [256, 128, 512], P('gx', 'gy', 'gz')
- arrived: float32 [16, 4, 2, 22, 6, 128], P('gx', 'gy', 'gz')
- arrived_partners: int32 [16, 4, 2, 4, 6, 128], P('gx', 'gy', 'gz')
Inputs may be any that keep to these rules, and one draw needn't show every extreme that they name: `partners`: -1 marks an empty history slot; otherwise the code is bin * 128 + slot with bin 0 for the particle's own bin and 1 to 6 for the bins at -x, +x, -y, +y, -z, +z; a code never names the particle itself. `departures`: an entry is a local slot index ((bx * 2 + by) * 2 + bz) * 128 + slot, or -1; a slot appears at most once on its device; in each direction the used entries come first; in every draw some device fills all 128 entries of some direction.
All inputs are finite; a program needn't handle non-finite values.
Results may differ from a plain program's by a relative error of at most 0.0003.
Values sent between devices are 32-bit elements; how exact they have to be, the bound alone decides.
A program may use at most 192 MiB of HBM per device.

v0:
```python
import functools
import math

import jax
import jax.numpy as jnp
from jax import lax
from jax.experimental import pallas as pl
from jax.experimental.pallas import tpu as pltpu
from jax.sharding import PartitionSpec as P

SUBSTEPS = 2
HIST = 4
BINS = 8
SLOTS = 128

normal_stiff = 100.0
normal_damp = 2.0
shear_stiff = 30.0
friction = 0.5
time_step = 0.05
drag_coeff = 0.8
gravity = 1.0
soft_length = 0.05
force_floor = 0.5
volume_coeff = 100.0
drag_weight = 1.0

NOBODY = -10.0
TINY = 1e-30
AXES = ("gx", "gy", "gz")
MESH = pl.DeviceIdType.MESH


def neighbour(direction):
    axis = AXES[direction // 2]
    size = lax.axis_size(axis)
    here = lax.axis_index(axis)
    if direction % 2 == 0:
        return {axis: lax.rem(here + size - 1, size)}, here > 0
    return {axis: lax.rem(here + 1, size)}, here < size - 1


def bin_bits():
    row = lax.broadcasted_iota(jnp.int32, (BINS, SLOTS), 0)
    return [lax.shift_right_logical(row, 2 - axis) & 1 for axis in range(3)]


def swapped(value, axis):
    step = 4 >> axis
    if axis == 0:
        return pltpu.roll(value, step, 0)
    upper = bin_bits()[axis] == 1
    return jnp.where(upper, pltpu.roll(value, step, 0), pltpu.roll(value, BINS - step, 0))


def live_mask(counts_ref):
    row = lax.broadcasted_iota(jnp.int32, (BINS, SLOTS), 0)
    slot = lax.broadcasted_iota(jnp.int32, (BINS, SLOTS), 1)
    limit = jnp.zeros((BINS, SLOTS), jnp.int32)
    for b in range(BINS):
        limit = jnp.where(row == b, counts_ref[b], limit)
    return slot < limit


def halves(value):
    high = value.astype(jnp.bfloat16).astype(jnp.float32)
    return high, value - high


def one_hot(index_row):
    rows = lax.broadcasted_iota(jnp.int32, (SLOTS, SLOTS), 0)
    return rows == index_row


def cross(a, b):
    return [
        a[1] * b[2] - a[2] * b[1],
        a[2] * b[0] - a[0] * b[2],
        a[0] * b[1] - a[1] * b[0],
    ]


def dot(a, b):
    return a[0] * b[0] + a[1] * b[1] + a[2] * b[2]


def pair_pass(columns_ref, table_ref, tables, sums_ref, first):
    def chunk(c, carry):
        start = pl.multiple_of(c * 8, 8)
        tile = columns_ref[pl.ds(start, 8), :]
        lane = lax.broadcasted_iota(jnp.int32, (8, SLOTS), 1)
        if first:
            result = jnp.zeros((8, SLOTS), jnp.float32)
        else:
            result = sums_ref[pl.ds(start, 8), :]
        for b in range(BINS):
            mine = [
                jnp.broadcast_to(tile[:, f * 8 + b : f * 8 + b + 1], (8, SLOTS)) for f in range(7)
            ]
            total = None
            for t in tables:
                other = [
                    jnp.broadcast_to(table_ref[t, f, b : b + 1, :], (8, SLOTS))
                    for f in (0, 1, 2, 3, 4, 5, 9)
                ]
                sep = [mine[i] - other[i] for i in range(3)]
                square = dot(sep, sep) + soft_length**2
                inverse = lax.rsqrt(square)
                overlap = mine[6] + other[6] - square * inverse
                delta = jnp.maximum(overlap, 0.0)
                root = delta * lax.rsqrt(jnp.maximum(overlap, TINY))
                vrel = [mine[3 + i] - other[3 + i] for i in range(3)]
                approach = dot(vrel, sep) * inverse
                weight = ((normal_stiff / normal_damp) * delta - approach) * (root * inverse)
                term = [weight * sep[i] for i in range(3)]
                total = term if total is None else [total[i] + term[i] for i in range(3)]
            for i in range(3):
                column = jnp.sum(total[i], axis=1, keepdims=True)
                fresh = result + column if not first else jnp.broadcast_to(column, (8, SLOTS))
                result = jnp.where(lane == i * 8 + b, fresh, result)
        sums_ref[pl.ds(start, 8), :] = result
        return carry

    lax.fori_loop(0, SLOTS // 8, chunk, 0)


def gathered(table_ref, tables, which, masks, member, got):
    for f in range(10):
        value = got[f]
        for t in tables:
            picked = jnp.take_along_axis(
                table_ref[t, f], member, axis=1, mode="promise_in_bounds"
            )
            value = jnp.where(masks[t], picked, value)
        got[f] = value
    return got


def particles(
    pos_ref,
    vel_ref,
    spin_ref,
    radii_ref,
    counts_ref,
    springs_ref,
    partners_ref,
    cells_ref,
    departures_ref,
    gas_hbm,
    pressure_hbm,
    state_out,
    springs_out,
    gas_out,
    moved_out,
    face_x_out,
    face_y_out,
    face_z_out,
    gas_ref,
    pressure_ref,
    table_ref,
    columns_ref,
    sums_ref,
    own_ref,
    halo_ref,
    own_2_ref,
    halo_2_ref,
    picked_ref,
    gone_ref,
    come_ref,
    send_y_ref,
    send_z_ref,
    face_x_ref,
    face_y_ref,
    face_z_ref,
    local_sem,
    send_sem,
    recv_sem,
):
    gas_copy = pltpu.make_async_copy(gas_hbm, gas_ref, local_sem.at[0])
    pressure_copy = pltpu.make_async_copy(pressure_hbm, pressure_ref, local_sem.at[1])
    gas_copy.start()
    pressure_copy.start()

    there = [neighbour(d) for d in range(6)]

    barrier = pltpu.get_barrier_semaphore()
    for d in range(6):

        @pl.when(there[d][1])
        def _():
            pl.semaphore_signal(barrier, inc=1, device_id=there[d][0], device_id_type=MESH)

    def halo_copy(d):
        return pltpu.make_async_remote_copy(
            src_ref=own_ref,
            dst_ref=halo_ref.at[d ^ 1],
            send_sem=send_sem.at[0, d],
            recv_sem=recv_sem.at[0, d ^ 1],
            device_id=there[d][0],
            device_id_type=MESH,
        )

    def halo_copy_2(d):
        return pltpu.make_async_remote_copy(
            src_ref=own_2_ref,
            dst_ref=halo_2_ref.at[d ^ 1],
            send_sem=send_sem.at[1, d],
            recv_sem=recv_sem.at[1, d ^ 1],
            device_id=there[d][0],
            device_id_type=MESH,
        )

    def moved_copy(d):
        return pltpu.make_async_remote_copy(
            src_ref=gone_ref.at[d],
            dst_ref=come_ref.at[d],
            send_sem=send_sem.at[2, d],
            recv_sem=recv_sem.at[2, d],
            device_id=there[d][0],
            device_id_type=MESH,
        )

    def face_copy(d):
        side = d % 2
        if d < 2:
            source = pressure_ref.at[0 if side == 0 else pressure_ref.shape[0] - 1]
            target = face_x_ref.at[1 - side]
        elif d < 4:
            source, target = send_y_ref.at[side], face_y_ref.at[1 - side]
        else:
            source, target = send_z_ref.at[side], face_z_ref.at[1 - side]
        return pltpu.make_async_remote_copy(
            src_ref=source,
            dst_ref=target,
            send_sem=send_sem.at[3, d],
            recv_sem=recv_sem.at[3, d ^ 1],
            device_id=there[d][0],
            device_id_type=MESH,
        )

    live = live_mask(counts_ref)
    radius = radii_ref[...]
    partner_radius = jnp.where(live, radius, NOBODY)
    for i in range(3):
        own_ref[i] = pos_ref[i]
        own_ref[3 + i] = vel_ref[i]
        own_ref[6 + i] = spin_ref[i]
    own_ref[9] = partner_radius

    for s in range(6):

        @pl.when(jnp.logical_not(there[s][1]))
        def _():
            halo_ref[s] = jnp.zeros((10, BINS, SLOTS), jnp.float32)
            halo_ref[s, 9] = jnp.full((BINS, SLOTS), NOBODY, jnp.float32)
            halo_2_ref[s] = jnp.zeros((9, BINS, SLOTS), jnp.float32)
            come_ref[s ^ 1] = jnp.zeros((32, SLOTS), jnp.float32)
            face = (face_x_ref, face_y_ref, face_z_ref)[s // 2]
            face[s % 2] = jnp.zeros(face.shape[1:], jnp.float32)

    pl.semaphore_wait(barrier, sum(there[d][1].astype(jnp.int32) for d in range(6)))

    for d in range(6):

        @pl.when(there[d][1])
        def _():
            halo_copy(d).start()

    pressure_copy.wait()
    cells_x, cells_y, cells_z = pressure_ref.shape
    lane = lax.broadcasted_iota(jnp.int32, (cells_y, SLOTS), 1)
    for side in range(2):
        send_y_ref[side] = pressure_ref[:, 0 if side == 0 else cells_y - 1, :]
        face = jnp.zeros((cells_y, SLOTS), jnp.float32)
        for x in range(cells_x):
            if side == 0:
                column = pressure_ref[x, :, 0:SLOTS][:, 0:1]
            else:
                column = pressure_ref[x, :, cells_z - SLOTS : cells_z][:, SLOTS - 1 : SLOTS]
            face = jnp.where(lane == x, jnp.broadcast_to(column, (cells_y, SLOTS)), face)
        send_z_ref[side] = face
    for d in range(6):

        @pl.when(there[d][1])
        def _():
            face_copy(d).start()

    bits = bin_bits()
    code = [partners_ref[k] for k in range(HIST)]
    valid = [jnp.where(code[k] >= 0, 1.0, 0.0) for k in range(HIST)]
    member = [jnp.maximum(code[k], 0) & (SLOTS - 1) for k in range(HIST)]
    which = [lax.shift_right_logical(jnp.maximum(code[k], 0), 7) for k in range(HIST)]

    def masks_of(k):
        found = [which[k] == 0]
        for axis in range(3):
            found.append(which[k] == 2 * axis + 2 - bits[axis])
        for axis in range(3):
            found.append(which[k] == 2 * axis + 1 + bits[axis])
        return found

    safe = jnp.where(radius > 0.0, radius, 1.0)
    mass = safe * 10.0
    mass = mass * mass * mass
    inertia = 0.4 * mass * safe * safe

    def inner_tables(fields):
        for f in range(10):
            table_ref[0, f] = fields[f]
            for axis in range(3):
                value = swapped(fields[f], axis)
                if f == axis:
                    value = value + jnp.where(bits[axis] == 0, 1.0, -1.0)
                table_ref[1 + axis, f] = value
        columns_ref[...] = jnp.concatenate(
            [fields[f] for f in range(6)] + [radius, jnp.zeros((72, SLOTS), jnp.float32)], axis=0
        ).T

    def outer_tables(ref, count):
        for axis in range(3):
            for f in range(count):
                value = jnp.where(
                    bits[axis] == 0,
                    swapped(ref[2 * axis, f], axis),
                    swapped(ref[2 * axis + 1, f], axis),
                )
                if f == axis:
                    value = value + jnp.where(bits[axis] == 0, -1.0, 1.0)
                table_ref[4 + axis, f] = value

    zero = jnp.zeros((BINS, SLOTS), jnp.float32)
    for step in range(SUBSTEPS):
        source = own_ref if step == 0 else own_2_ref
        fields = [source[f] for f in range(9)] + [partner_radius]
        inner_tables(fields)
        pair_pass(columns_ref, table_ref, (0, 1, 2, 3), sums_ref, True)

        if step == 0:
            gas_copy.wait()
            for b in range(BINS):
                bx, by, bz = b // 4, b // 2 % 2, b % 2
                size_x, size_y = cells_x // 2, cells_y // 2
                block = gas_ref[
                    :,
                    bx * size_x : (bx + 1) * size_x,
                    by * size_y : (by + 1) * size_y,
                    bz * SLOTS : (bz + 1) * SLOTS,
                ].reshape(3 * SLOTS, SLOTS)
                cell = cells_ref[b : b + 1, :]
                high, low = halves(block)
                left = jnp.concatenate(
                    [high.astype(jnp.bfloat16), low.astype(jnp.bfloat16)], axis=1
                )
                lanes = jnp.where(one_hot(cell & (SLOTS - 1)), 1.0, 0.0).astype(jnp.bfloat16)
                right = jnp.concatenate([lanes, lanes], axis=0)
                product = jnp.dot(left, right, preferred_element_type=jnp.float32)
                rows = one_hot(lax.shift_right_logical(cell, 7))
                for i in range(3):
                    gas_out[i, b : b + 1, :] = jnp.sum(
                        jnp.where(rows, product[i * SLOTS : (i + 1) * SLOTS], 0.0),
                        axis=0,
                        keepdims=True,
                    )

        for d in range(6):

            @pl.when(there[d][1])
            def _():
                (halo_copy if step == 0 else halo_copy_2)(d ^ 1).wait_recv()

        outer_tables(halo_ref if step == 0 else halo_2_ref, 10 if step == 0 else 9)
        pair_pass(columns_ref, table_ref, (4, 5, 6), sums_ref, False)
        normal = sums_ref[...].T

        places, speeds, turning = fields[0:3], fields[3:6], fields[6:9]
        spring_source = springs_ref if step == 0 else springs_out
        shear_sum = [zero] * 3
        torque_sum = [zero] * 3
        for k in range(HIST):
            other = gathered(
                table_ref, range(7), which[k], masks_of(k), member[k], [zero] * 10
            )
            sep = [places[i] - other[i] for i in range(3)]
            square = dot(sep, sep) + soft_length**2
            inverse = lax.rsqrt(square)
            unit = [sep[i] * inverse for i in range(3)]
            overlap = radius + other[9] - square * inverse
            delta = jnp.maximum(overlap, 0.0)
            root = delta * lax.rsqrt(jnp.maximum(overlap, TINY))
            relative = [speeds[i] - other[3 + i] for i in range(3)]
            approach = dot(relative, unit)
            pressing = root * (normal_stiff * delta - normal_damp * approach)
            lever = [radius * turning[i] + other[9] * other[6 + i] for i in range(3)]
            spun = cross(lever, unit)
            contact = [relative[i] - spun[i] for i in range(3)]
            along = dot(contact, unit)
            sliding = [contact[i] - along * unit[i] for i in range(3)]
            spring = [spring_source[i * HIST + k] for i in range(3)]
            tilt = dot(spring, unit)
            stretched = [
                spring[i] - tilt * unit[i] + time_step * sliding[i] for i in range(3)
            ]
            length = jnp.sqrt(dot(stretched, stretched))
            limit = jnp.minimum(
                1.0, friction * jnp.abs(pressing) / jnp.maximum(shear_stiff * length, force_floor)
            )
            scale = valid[k] * limit
            fresh = [scale * stretched[i] for i in range(3)]
            shear = [-shear_stiff * fresh[i] for i in range(3)]
            twist = cross(shear, unit)
            for i in range(3):
                springs_out[i * HIST + k] = fresh[i]
            shear_sum = [shear_sum[i] + shear[i] for i in range(3)]
            torque_sum = [torque_sum[i] + twist[i] for i in range(3)]

        for i in range(3):
            push = normal_damp * normal[i * 8 : i * 8 + 8, :] + shear_sum[i]
            push = push + drag_coeff * (gas_out[i] - speeds[i])
            speed = speeds[i] + time_step * (push / mass - (gravity if i == 2 else 0.0))
            spin = turning[i] + time_step * (radius * torque_sum[i]) / inertia
            target = own_2_ref if step == 0 else state_out
            target[3 + i] = speed
            target[6 + i] = spin
            target[i] = places[i] + time_step * speed
        if step == 0:
            for d in range(6):

                @pl.when(there[d][1])
                def _():
                    halo_copy_2(d).start()

    for f in range(9):
        picked_ref[:, f, :] = state_out[f]
    picked_ref[:, 9, :] = radius
    for f in range(3 * HIST):
        picked_ref[:, 10 + f, :] = springs_out[f]
    for k in range(HIST):
        picked_ref[:, 22 + k, :] = (code[k] + 1).astype(jnp.float32)
    for f in range(26, 32):
        picked_ref[:, f, :] = zero
    for d in range(6):
        entry = jnp.broadcast_to(departures_ref[d : d + 1, :], (8, SLOTS))
        slot = entry & (SLOTS - 1)
        home = lax.shift_right_arithmetic(entry, 7)
        for g in range(4):
            value = zero
            for b in range(BINS):
                taken = jnp.take_along_axis(
                    picked_ref[b, g * 8 : g * 8 + 8, :], slot, axis=1, mode="promise_in_bounds"
                )
                value = jnp.where(home == b, taken, value)
            gone_ref[d, g * 8 : g * 8 + 8, :] = value

        @pl.when(there[d][1])
        def _():
            moved_copy(d).start()

    for d in range(6):

        @pl.when(there[d][1])
        def _():
            halo_copy(d).wait_send()
            halo_copy_2(d).wait_send()
            face_copy(d).wait_send()
            face_copy(d ^ 1).wait_recv()

    face_x_out[...] = face_x_ref[...]
    face_y_out[...] = face_y_ref[...]
    face_z_out[...] = face_z_ref[...]

    for d in range(6):

        @pl.when(there[d][1])
        def _():
            moved_copy(d).wait_send()
            moved_copy(d ^ 1).wait_recv()

    moved_out[...] = come_ref[...]


def finish(
    state_ref,
    springs_ref,
    gas_ref,
    radii_ref,
    counts_ref,
    cells_ref,
    moved_ref,
    pressure_ref,
    source_ref,
    face_x_ref,
    face_y_ref,
    face_z_ref,
    pos_out,
    vel_out,
    spin_out,
    springs_out,
    force_out,
    pressure_out,
    arrived_out,
    codes_out,
):
    for i in range(3):
        pos_out[i] = state_ref[i]
        vel_out[i] = state_ref[3 + i]
        spin_out[i] = state_ref[6 + i]
    springs_out[...] = springs_ref[...]
    for d in range(6):
        arrived_out[:, d, :] = moved_ref[d, 0:22, :]
        codes_out[:, d, :] = moved_ref[d, 22:26, :].astype(jnp.int32) - 1

    cells_x, cells_y, cells_z = pressure_ref.shape
    row = lax.broadcasted_iota(jnp.int32, (cells_y, cells_z), 0)
    lane = lax.broadcasted_iota(jnp.int32, (cells_y, cells_z), 1)
    for x in range(cells_x):
        here = pressure_ref[x]
        total = pressure_ref[x - 1] if x > 0 else face_x_ref[0]
        total = total + (pressure_ref[x + 1] if x < cells_x - 1 else face_x_ref[1])
        total = total + jnp.where(row == 0, face_y_ref[0, x : x + 1, :], pltpu.roll(here, 1, 0))
        total = total + jnp.where(
            row == cells_y - 1, face_y_ref[1, x : x + 1, :], pltpu.roll(here, cells_y - 1, 0)
        )
        total = total + jnp.where(
            lane == 0,
            jnp.broadcast_to(face_z_ref[0][:, x : x + 1], here.shape),
            pltpu.roll(here, 1, 1),
        )
        total = total + jnp.where(
            lane == cells_z - 1,
            jnp.broadcast_to(face_z_ref[1][:, x : x + 1], here.shape),
            pltpu.roll(here, cells_z - 1, 1),
        )
        pressure_out[x] = total + source_ref[x]

    live = jnp.where(live_mask(counts_ref), 1.0, 0.0)
    radius = radii_ref[...]
    values = [drag_coeff * (state_ref[3 + i] - gas_ref[i]) * live for i in range(3)]
    values.append(4.0 / 3.0 * math.pi * (radius * radius * radius) * live)
    values = [halves(value) for value in values]
    size_x, size_y = cells_x // 2, cells_y // 2
    for b in range(BINS):
        bx, by, bz = b // 4, b // 2 % 2, b % 2
        block = (
            slice(bx * size_x, (bx + 1) * size_x),
            slice(by * size_y, (by + 1) * size_y),
            slice(bz * SLOTS, (bz + 1) * SLOTS),
        )
        cell = cells_ref[b : b + 1, :]
        rows = one_hot(lax.shift_right_logical(cell, 7))
        lanes = jnp.where(one_hot(cell & (SLOTS - 1)), 1.0, 0.0).astype(jnp.bfloat16)
        right = jnp.concatenate([lanes, lanes], axis=1)
        left = jnp.concatenate(
            [
                jnp.concatenate(
                    [
                        jnp.where(rows, part[b : b + 1, :], 0.0).astype(jnp.bfloat16)
                        for part in value
                    ],
                    axis=1,
                )
                for value in values
            ],
            axis=0,
        )
        product = lax.dot_general(
            left, right, (((1,), (1,)), ((), ())), preferred_element_type=jnp.float32
        )
        parts = [
            product[i * SLOTS : (i + 1) * SLOTS].reshape(size_x, size_y, SLOTS) for i in range(4)
        ]
        for i in range(3):
            force_out[(i,) + block] = parts[i]
        pressure_out[block] = (
            pressure_out[block] + volume_coeff * parts[3] + drag_weight * parts[2]
        ) / 6.0


def body(
    positions,
    velocities,
    spins,
    radii,
    counts,
    springs,
    partners,
    cells,
    departures,
    fluid_velocity,
    pressure,
    pressure_source,
):
    cells_x, cells_y, cells_z = pressure.shape
    f32 = jnp.float32
    vmem = pl.BlockSpec(memory_space=pltpu.VMEM)
    smem = pl.BlockSpec(memory_space=pltpu.SMEM)
    anywhere = pl.BlockSpec(memory_space=pl.ANY)
    shape = jax.ShapeDtypeStruct
    rows = (BINS, SLOTS)
    radii_rows = radii.reshape(rows)
    cells_rows = cells.reshape(rows)
    counts_row = counts.reshape(BINS)
    state, new_springs, gas, moved, face_x, face_y, face_z = pl.pallas_call(
        particles,
        out_shape=(
            shape((9,) + rows, f32),
            shape((3 * HIST,) + rows, f32),
            shape((3,) + rows, f32),
            shape((6, 32, SLOTS), f32),
            shape((2, cells_y, cells_z), f32),
            shape((2, cells_x, cells_z), f32),
            shape((2, cells_y, SLOTS), f32),
        ),
        in_specs=[vmem] * 4 + [smem] + [vmem] * 4 + [anywhere] * 2,
        out_specs=(vmem,) * 7,
        scratch_shapes=[
            pltpu.VMEM(fluid_velocity.shape, f32),
            pltpu.VMEM(pressure.shape, f32),
            pltpu.VMEM((7, 10) + rows, f32),
            pltpu.VMEM((SLOTS, SLOTS), f32),
            pltpu.VMEM((SLOTS, SLOTS), f32),
            pltpu.VMEM((10,) + rows, f32),
            pltpu.VMEM((6, 10) + rows, f32),
            pltpu.VMEM((9,) + rows, f32),
            pltpu.VMEM((6, 9) + rows, f32),
            pltpu.VMEM((BINS, 32, SLOTS), f32),
            pltpu.VMEM((6, 32, SLOTS), f32),
            pltpu.VMEM((6, 32, SLOTS), f32),
            pltpu.VMEM((2, cells_x, cells_z), f32),
            pltpu.VMEM((2, cells_y, SLOTS), f32),
            pltpu.VMEM((2, cells_y, cells_z), f32),
            pltpu.VMEM((2, cells_x, cells_z), f32),
            pltpu.VMEM((2, cells_y, SLOTS), f32),
            pltpu.SemaphoreType.DMA((2,)),
            pltpu.SemaphoreType.DMA((4, 6)),
            pltpu.SemaphoreType.DMA((4, 6)),
        ],
        compiler_params=pltpu.CompilerParams(
            collective_id=0, has_side_effects=True, vmem_limit_bytes=32 * 1024 * 1024
        ),
    )(
        positions.reshape((3,) + rows),
        velocities.reshape((3,) + rows),
        spins.reshape((3,) + rows),
        radii_rows,
        counts_row,
        springs.reshape((3 * HIST,) + rows),
        partners.reshape((HIST,) + rows),
        cells_rows,
        departures.reshape(6, SLOTS),
        fluid_velocity,
        pressure,
    )
    places, speeds, turning, last_springs, force, new_pressure, arrived, codes = pl.pallas_call(
        finish,
        out_shape=(
            shape((3,) + rows, f32),
            shape((3,) + rows, f32),
            shape((3,) + rows, f32),
            shape((3 * HIST,) + rows, f32),
            shape(fluid_velocity.shape, f32),
            shape(pressure.shape, f32),
            shape((22, 6, SLOTS), f32),
            shape((4, 6, SLOTS), jnp.int32),
        ),
        in_specs=[vmem] * 4 + [smem] + [vmem] * 7,
        out_specs=(vmem,) * 8,
        compiler_params=pltpu.CompilerParams(vmem_limit_bytes=32 * 1024 * 1024),
    )(
        state,
        new_springs,
        gas,
        radii_rows,
        counts_row,
        cells_rows,
        moved,
        pressure,
        pressure_source,
        face_x,
        face_y,
        face_z,
    )
    return (
        places.reshape(positions.shape),
        speeds.reshape(positions.shape),
        turning.reshape(positions.shape),
        last_springs.reshape(springs.shape),
        force,
        new_pressure,
        arrived[None, None, None],
        codes[None, None, None],
    )


def solution(mesh):
    return jax.shard_map(
        body,
        mesh=mesh,
        in_specs=(
            P(None, "gx", "gy", "gz", None),
            P(None, "gx", "gy", "gz", None),
            P(None, "gx", "gy", "gz", None),
            P("gx", "gy", "gz", None),
            P("gx", "gy", "gz"),
            P(None, None, "gx", "gy", "gz", None),
            P(None, "gx", "gy", "gz", None),
            P("gx", "gy", "gz", None),
            P("gx", "gy", "gz", None, None),
            P(None, "gx", "gy", "gz"),
            P("gx", "gy", "gz"),
            P("gx", "gy", "gz"),
        ),
        out_specs=(
            P(None, "gx", "gy", "gz", None),
            P(None, "gx", "gy", "gz", None),
            P(None, "gx", "gy", "gz", None),
            P(None, None, "gx", "gy", "gz", None),
            P(None, "gx", "gy", "gz"),
            P("gx", "gy", "gz"),
            P("gx", "gy", "gz", None, None, None),
            P("gx", "gy", "gz", None, None, None),
        ),
        check_vma=False,
    )
```

profile of v0, /device:TPU:1, one launch (start us, length us, event | category | flops | bytes accessed | tf_op | source)
XLA Modules:
  0.0 60.5 jit_solution(4051898684223623774)
XLA Ops:
  0.6 0.8 %reshape.59.counts_ref = s32[8]{0:T(128)S(1)} reshape(s32[2,2,2]{2,1,0:T(2,128)} %param.16) | data formatting | bytes 64 | tf_op jit(solution)/shard_map/reshape | solution.py:601
  1.4 0.7 %copy.24 = s32[1,1,1,6,128]{4,3,2,1,0:T(8,128)S(1)} copy(s32[1,1,1,6,128]{4,2,3,1,0:T(1,128)} %param.20) | data formatting | bytes 6144
  2.1 0.0 copy-start
  2.1 1.0 %copy-done = f32[16,32,256]{2,1,0:T(8,128)S(1)} copy-done((f32[16,32,256]{2,1,0:T(8,128)S(1)}, f32[16,32,256]{2,1,0:T(8,128)}, u32[]{:S(2)}) %copy-start) | copy-done | bytes 524312
  3.1 0.0 copy-start.1
  3.1 1.4 %copy-done.1 = f32[3,16,32,256]{3,2,1,0:T(8,128)S(1)} copy-done((f32[3,16,32,256]{3,2,1,0:T(8,128)S(1)}, f32[3,16,32,256]{3,2,1,0:T(8,128)}, u32[]{:S(2)}) %copy-start.1) | copy-done | bytes 1572888
  4.5 0.0 copy-start.3
  4.5 0.8 %copy-done.3 = f32[3,4,2,2,2,128]{5,4,3,2,1,0:T(2,128)S(1)} copy-done((f32[3,4,2,2,2,128]{5,4,3,2,1,0:T(2,128)S(1)}, f32[3,4,2,2,2,128]{5,4,3,2,1,0:T(2,128)}, u32[]{:S(2)}) %copy-start.3) | copy-done | bytes 49176
  5.3 0.0 copy-start.4
  5.3 0.7 %copy-done.4 = s32[4,2,2,2,128]{4,3,2,1,0:T(2,128)S(1)} copy-done((s32[4,2,2,2,128]{4,3,2,1,0:T(2,128)S(1)}, s32[4,2,2,2,128]{4,3,2,1,0:T(2,128)}, u32[]{:S(2)}) %copy-start.4) | copy-done | bytes 16408
  6.1 0.0 copy-start.5
  6.1 0.7 %copy-done.5 = f32[2,2,2,128]{3,2,1,0:T(2,128)S(1)} copy-done((f32[2,2,2,128]{3,2,1,0:T(2,128)S(1)}, f32[2,2,2,128]{3,2,1,0:T(2,128)}, u32[]{:S(2)}) %copy-start.5) | copy-done | bytes 4120
  6.7 0.0 copy-start.6
  6.7 0.7 %copy-done.6 = s32[2,2,2,128]{3,2,1,0:T(2,128)S(1)} copy-done((s32[2,2,2,128]{3,2,1,0:T(2,128)S(1)}, s32[2,2,2,128]{3,2,1,0:T(2,128)}, u32[]{:S(2)}) %copy-start.6) | copy-done | bytes 4120
  7.4 0.0 copy-start.7
  7.4 0.7 %copy-done.7 = f32[3,2,2,2,128]{4,3,2,1,0:T(2,128)S(1)} copy-done((f32[3,2,2,2,128]{4,3,2,1,0:T(2,128)S(1)}, f32[3,2,2,2,128]{4,3,2,1,0:T(2,128)}, u32[]{:S(2)}) %copy-start.7) | copy-done | bytes 12312
  8.1 0.0 copy-start.8
  8.1 0.7 %copy-done.8 = f32[3,2,2,2,128]{4,3,2,1,0:T(2,128)S(1)} copy-done((f32[3,2,2,2,128]{4,3,2,1,0:T(2,128)S(1)}, f32[3,2,2,2,128]{4,3,2,1,0:T(2,128)}, u32[]{:S(2)}) %copy-start.8) | copy-done | bytes 12312
  8.8 0.0 copy-start.9
  8.8 0.7 %copy-done.9 = f32[3,2,2,2,128]{4,3,2,1,0:T(2,128)S(1)} copy-done((f32[3,2,2,2,128]{4,3,2,1,0:T(2,128)S(1)}, f32[3,2,2,2,128]{4,3,2,1,0:T(2,128)}, u32[]{:S(2)}) %copy-start.9) | copy-done | bytes 12312
  9.5 0.0 copy-start.2
  9.5 46.9 %shard_map.179 = (f32[9,8,128]{2,1,0:T(8,128)S(1)}, f32[12,8,128]{2,1,0:T(8,128)S(1)}, f32[3,8,128]{2,1,0:T(8,128)S(1)}, f32[6,32,128]{2,1,0:T(8,128)S(1)}, f32[...) custom-call(f32[3,8,128]{2,1,0:T(8,128)S(1)} %bitcast.25, f32[3,8,128]{2,1,0:T(8,128)S(1)} %bitcast.26, ...), custom_call_target="tpu_custom_call" | custom-call | tf_op jit(solution)/shard_map/pallas_call | solution.py:602
  56.4 0.0 copy-done.2
  56.5 2.7 %shard_map.180 = (f32[3,8,128]{2,1,0:T(8,128)}, f32[3,8,128]{2,1,0:T(8,128)}, f32[3,8,128]{2,1,0:T(8,128)}, f32[12,8,128]{2,1,0:T(8,128)}, f32[3,16,32,256]{3,2,...) custom-call(f32[9,8,128]{2,1,0:T(8,128)S(1)} %get-tuple-element.23.state_ref, ...), custom_call_target="tpu_custom_call" | custom-call | tf_op jit(solution)/shard_map/pallas_call | solution.py:653
  59.2 0.6 copy.21
  59.8 0.7 %copy.20 = f32[1,1,1,22,6,128]{5,2,4,3,1,0:T(1,128)} copy(f32[1,1,1,22,6,128]{5,4,3,2,1,0:T(8,128)S(1)} %bitcast.16) | data formatting | bytes 135168
Async XLA Ops:
  2.1 1.0 %copy-start = (f32[16,32,256]{2,1,0:T(8,128)S(1)}, f32[16,32,256]{2,1,0:T(8,128)}, u32[]{:S(2)}) copy-start(f32[16,32,256]{2,1,0:T(8,128)} %pressure_ref.1) | copy-start | bytes 1572868
  3.1 1.4 %copy-start.1 = (f32[3,16,32,256]{3,2,1,0:T(8,128)S(1)}, f32[3,16,32,256]{3,2,1,0:T(8,128)}, u32[]{:S(2)}) copy-start(f32[3,16,32,256]{3,2,1,0:T(8,128)} %gas_hbm.1) | copy-start | bytes 4718596
  4.5 0.8 %copy-start.3 = (f32[3,4,2,2,2,128]{5,4,3,2,1,0:T(2,128)S(1)}, f32[3,4,2,2,2,128]{5,4,3,2,1,0:T(2,128)}, u32[]{:S(2)}) copy-start(f32[3,4,2,2,2,128]{5,4,3,2,1,0:T(2,128)} %param.17) | copy-start | bytes 147460
  5.3 0.7 %copy-start.4 = (s32[4,2,2,2,128]{4,3,2,1,0:T(2,128)S(1)}, s32[4,2,2,2,128]{4,3,2,1,0:T(2,128)}, u32[]{:S(2)}) copy-start(s32[4,2,2,2,128]{4,3,2,1,0:T(2,128)} %param.18) | copy-start | bytes 49156
  6.1 0.7 %copy-start.5 = (f32[2,2,2,128]{3,2,1,0:T(2,128)S(1)}, f32[2,2,2,128]{3,2,1,0:T(2,128)}, u32[]{:S(2)}) copy-start(f32[2,2,2,128]{3,2,1,0:T(2,128)} %param.15) | copy-start | bytes 12292
  6.7 0.7 %copy-start.6 = (s32[2,2,2,128]{3,2,1,0:T(2,128)S(1)}, s32[2,2,2,128]{3,2,1,0:T(2,128)}, u32[]{:S(2)}) copy-start(s32[2,2,2,128]{3,2,1,0:T(2,128)} %param.19) | copy-start | bytes 12292
  7.4 0.7 %copy-start.7 = (f32[3,2,2,2,128]{4,3,2,1,0:T(2,128)S(1)}, f32[3,2,2,2,128]{4,3,2,1,0:T(2,128)}, u32[]{:S(2)}) copy-start(f32[3,2,2,2,128]{4,3,2,1,0:T(2,128)} %param.12) | copy-start | bytes 36868
  8.1 0.7 %copy-start.8 = (f32[3,2,2,2,128]{4,3,2,1,0:T(2,128)S(1)}, f32[3,2,2,2,128]{4,3,2,1,0:T(2,128)}, u32[]{:S(2)}) copy-start(f32[3,2,2,2,128]{4,3,2,1,0:T(2,128)} %param.13) | copy-start | bytes 36868
  8.8 0.7 %copy-start.9 = (f32[3,2,2,2,128]{4,3,2,1,0:T(2,128)S(1)}, f32[3,2,2,2,128]{4,3,2,1,0:T(2,128)}, u32[]{:S(2)}) copy-start(f32[3,2,2,2,128]{4,3,2,1,0:T(2,128)} %param.14) | copy-start | bytes 36868
  9.5 46.9 %copy-start.2 = (f32[16,32,256]{2,1,0:T(8,128)S(1)}, f32[16,32,256]{2,1,0:T(8,128)}, u32[]{:S(2)}) copy-start(f32[16,32,256]{2,1,0:T(8,128)} %source_ref.1) | copy-start | bytes 1572868
where the time goes:
time: 61 us; the launch traced here: 60.5 us
  Pallas kernels  49.6 us (81%)
  local copies, waits for them, and re-layouts  10.2 us (17%)
  between operations  0.66 us (1%)
    pallas_call x1, Pallas kernels, body(): pl.pallas_call(particles, out_shape=(shape((9,) + rows, f32), shape((3 *...  46.9 us
    unnamed x23, local copies, waits for them, and re-layouts  9.45 us
    pallas_call x1, Pallas kernels, body(): pl.pallas_call(finish, out_shape=(shape((3,) + rows, f32), shape((3,) + r...  2.7 us

commit v1 on v0

--- a/solution.py
+++ b/solution.py
@@ -12,6 +12,7 @@
 HIST = 4
 BINS = 8
 SLOTS = 128
+VMEM_LIMIT = 64 * 1024 * 1024
 
 normal_stiff = 100.0
 normal_damp = 2.0
@@ -58,7 +59,7 @@
     slot = lax.broadcasted_iota(jnp.int32, (BINS, SLOTS), 1)
     limit = jnp.zeros((BINS, SLOTS), jnp.int32)
     for b in range(BINS):
-        limit = jnp.where(row == b, counts_ref[b], limit)
+        limit = jnp.where(row == b, counts_ref[b // 4, b // 2 % 2, b % 2], limit)
     return slot < limit
 
 
@@ -84,20 +85,23 @@
     return a[0] * b[0] + a[1] * b[1] + a[2] * b[2]
 
 
-def pair_pass(columns_ref, table_ref, tables, sums_ref, first):
+def pair_pass(columns_ref, mine_ref, table_ref, tables, sums_ref, first):
     def chunk(c, carry):
         start = pl.multiple_of(c * 8, 8)
-        tile = columns_ref[pl.ds(start, 8), :]
-        lane = lax.broadcasted_iota(jnp.int32, (8, SLOTS), 1)
-        if first:
-            result = jnp.zeros((8, SLOTS), jnp.float32)
-        else:
-            result = sums_ref[pl.ds(start, 8), :]
+        rows = pl.ds(start, 8)
+        tile = columns_ref[rows, :] if first else None
         for b in range(BINS):
-            mine = [
-                jnp.broadcast_to(tile[:, f * 8 + b : f * 8 + b + 1], (8, SLOTS)) for f in range(7)
-            ]
-            total = None
+            if first:
+                mine = [
+                    jnp.broadcast_to(tile[:, f * 8 + b : f * 8 + b + 1], (8, SLOTS))
+                    for f in range(7)
+                ]
+                for f in range(7):
+                    mine_ref[f, b, rows, :] = mine[f]
+                total = None
+            else:
+                mine = [mine_ref[f, b, rows, :] for f in range(7)]
+                total = [sums_ref[i, b, rows, :] for i in range(3)]
             for t in tables:
                 other = [
                     jnp.broadcast_to(table_ref[t, f, b : b + 1, :], (8, SLOTS))
@@ -115,13 +119,23 @@
                 term = [weight * sep[i] for i in range(3)]
                 total = term if total is None else [total[i] + term[i] for i in range(3)]
             for i in range(3):
-                column = jnp.sum(total[i], axis=1, keepdims=True)
-                fresh = result + column if not first else jnp.broadcast_to(column, (8, SLOTS))
-                result = jnp.where(lane == i * 8 + b, fresh, result)
-        sums_ref[pl.ds(start, 8), :] = result
+                sums_ref[i, b, rows, :] = total[i]
         return carry
 
     lax.fori_loop(0, SLOTS // 8, chunk, 0)
+
+
+def lane_sums(sums_ref, i):
+    row = lax.broadcasted_iota(jnp.int32, (BINS, 2 * SLOTS), 0)
+    total = jnp.zeros((BINS, SLOTS), jnp.float32)
+    for b in range(BINS):
+        high, low = halves(sums_ref[i, b])
+        right = jnp.concatenate([high.astype(jnp.bfloat16), low.astype(jnp.bfloat16)], axis=1)
+        left = jnp.where(row == b, 1.0, 0.0).astype(jnp.bfloat16)
+        total = total + lax.dot_general(
+            left, right, (((1,), (1,)), ((), ())), preferred_element_type=jnp.float32
+        )
+    return total
 
 
 def gathered(table_ref, tables, which, masks, member, got):
@@ -137,28 +151,40 @@
 
 
 def particles(
+    counts_ref,
+    pos_hbm,
+    vel_hbm,
+    spin_hbm,
+    radii_hbm,
+    springs_hbm,
+    partners_hbm,
+    cells_hbm,
+    departures_hbm,
+    gas_hbm,
+    pressure_hbm,
+    state_hbm,
+    new_springs_hbm,
+    u_hbm,
+    moved_hbm,
+    face_x_hbm,
+    face_y_hbm,
+    face_z_hbm,
+    state_out,
+    springs_out,
+    gas_out,
     pos_ref,
     vel_ref,
     spin_ref,
     radii_ref,
-    counts_ref,
     springs_ref,
     partners_ref,
     cells_ref,
     departures_ref,
-    gas_hbm,
-    pressure_hbm,
-    state_out,
-    springs_out,
-    gas_out,
-    moved_out,
-    face_x_out,
-    face_y_out,
-    face_z_out,
     gas_ref,
     pressure_ref,
     table_ref,
     columns_ref,
+    mine_ref,
     sums_ref,
     own_ref,
     halo_ref,
@@ -173,13 +199,29 @@
     face_y_ref,
     face_z_ref,
     local_sem,
+    store_sem,
     send_sem,
     recv_sem,
 ):
-    gas_copy = pltpu.make_async_copy(gas_hbm, gas_ref, local_sem.at[0])
-    pressure_copy = pltpu.make_async_copy(pressure_hbm, pressure_ref, local_sem.at[1])
-    gas_copy.start()
-    pressure_copy.start()
+    loads = [
+        pltpu.make_async_copy(source, target, local_sem.at[n])
+        for n, (source, target) in enumerate(
+            (
+                (pos_hbm, pos_ref),
+                (vel_hbm, vel_ref),
+                (spin_hbm, spin_ref),
+                (radii_hbm, radii_ref),
+                (pressure_hbm, pressure_ref),
+                (partners_hbm, partners_ref),
+                (springs_hbm, springs_ref),
+                (cells_hbm, cells_ref),
+                (departures_hbm, departures_ref),
+                (gas_hbm, gas_ref),
+            )
+        )
+    ]
+    for load in loads:
+        load.start()
 
     there = [neighbour(d) for d in range(6)]
 
@@ -238,6 +280,8 @@
             device_id_type=MESH,
         )
 
+    for load in loads[:4]:
+        load.wait()
     live = live_mask(counts_ref)
     radius = radii_ref[...]
     partner_radius = jnp.where(live, radius, NOBODY)
@@ -266,7 +310,8 @@
         def _():
             halo_copy(d).start()
 
-    pressure_copy.wait()
+    for load in loads[4:9]:
+        load.wait()
     cells_x, cells_y, cells_z = pressure_ref.shape
     lane = lax.broadcasted_iota(jnp.int32, (cells_y, SLOTS), 1)
     for side in range(2):
@@ -333,10 +378,10 @@
         source = own_ref if step == 0 else own_2_ref
         fields = [source[f] for f in range(9)] + [partner_radius]
         inner_tables(fields)
-        pair_pass(columns_ref, table_ref, (0, 1, 2, 3), sums_ref, True)
+        pair_pass(columns_ref, mine_ref, table_ref, (0, 1, 2, 3), sums_ref, True)
 
         if step == 0:
-            gas_copy.wait()
+            loads[9].wait()
             for b in range(BINS):
                 bx, by, bz = b // 4, b // 2 % 2, b % 2
                 size_x, size_y = cells_x // 2, cells_y // 2
@@ -369,8 +414,8 @@
                 (halo_copy if step == 0 else halo_copy_2)(d ^ 1).wait_recv()
 
         outer_tables(halo_ref if step == 0 else halo_2_ref, 10 if step == 0 else 9)
-        pair_pass(columns_ref, table_ref, (4, 5, 6), sums_ref, False)
-        normal = sums_ref[...].T
+        pair_pass(columns_ref, mine_ref, table_ref, (4, 5, 6), sums_ref, False)
+        normal = [lane_sums(sums_ref, i) for i in range(3)]
 
         places, speeds, turning = fields[0:3], fields[3:6], fields[6:9]
         spring_source = springs_ref if step == 0 else springs_out
@@ -414,7 +459,7 @@
             torque_sum = [torque_sum[i] + twist[i] for i in range(3)]
 
         for i in range(3):
-            push = normal_damp * normal[i * 8 : i * 8 + 8, :] + shear_sum[i]
+            push = normal_damp * normal[i] + shear_sum[i]
             push = push + drag_coeff * (gas_out[i] - speeds[i])
             speed = speeds[i] + time_step * (push / mass - (gravity if i == 2 else 0.0))
             spin = turning[i] + time_step * (radius * torque_sum[i]) / inertia
@@ -428,6 +473,23 @@
                 @pl.when(there[d][1])
                 def _():
                     halo_copy_2(d).start()
+
+    stores = [
+        pltpu.make_async_copy(source, target, store_sem.at[n])
+        for n, (source, target) in enumerate(
+            (
+                (state_out, state_hbm),
+                (springs_out, new_springs_hbm),
+                (gas_out, u_hbm),
+                (face_x_ref, face_x_hbm),
+                (face_y_ref, face_y_hbm),
+                (face_z_ref, face_z_hbm),
+                (come_ref, moved_hbm),
+            )
+        )
+    ]
+    for store in stores[:3]:
+        store.start()
 
     for f in range(9):
         picked_ref[:, f, :] = state_out[f]
@@ -439,7 +501,7 @@
     for f in range(26, 32):
         picked_ref[:, f, :] = zero
     for d in range(6):
-        entry = jnp.broadcast_to(departures_ref[d : d + 1, :], (8, SLOTS))
+        entry = jnp.broadcast_to(departures_ref[d], (8, SLOTS))
         slot = entry & (SLOTS - 1)
         home = lax.shift_right_arithmetic(entry, 7)
         for g in range(4):
@@ -464,9 +526,8 @@
             face_copy(d).wait_send()
             face_copy(d ^ 1).wait_recv()
 
-    face_x_out[...] = face_x_ref[...]
-    face_y_out[...] = face_y_ref[...]
-    face_z_out[...] = face_z_ref[...]
+    for store in stores[3:6]:
+        store.start()
 
     for d in range(6):
 
@@ -475,22 +536,24 @@
             moved_copy(d).wait_send()
             moved_copy(d ^ 1).wait_recv()
 
-    moved_out[...] = come_ref[...]
+    stores[6].start()
+    for store in stores:
+        store.wait()
 
 
 def finish(
-    state_ref,
-    springs_ref,
-    gas_ref,
-    radii_ref,
     counts_ref,
-    cells_ref,
-    moved_ref,
-    pressure_ref,
-    source_ref,
-    face_x_ref,
-    face_y_ref,
-    face_z_ref,
+    state_hbm,
+    springs_hbm,
+    gas_hbm,
+    radii_hbm,
+    cells_hbm,
+    moved_hbm,
+    pressure_hbm,
+    source_hbm,
+    face_x_hbm,
+    face_y_hbm,
+    face_z_hbm,
     pos_out,
     vel_out,
     spin_out,
@@ -499,45 +562,73 @@
     pressure_out,
     arrived_out,
     codes_out,
+    speed_ref,
+    gas_ref,
+    radii_ref,
+    cells_ref,
+    moved_ref,
+    pressure_ref,
+    source_ref,
+    face_x_ref,
+    face_y_ref,
+    face_z_ref,
+    force_ref,
+    result_ref,
+    arrived_ref,
+    codes_ref,
+    load_sem,
+    store_sem,
 ):
-    for i in range(3):
-        pos_out[i] = state_ref[i]
-        vel_out[i] = state_ref[3 + i]
-        spin_out[i] = state_ref[6 + i]
-    springs_out[...] = springs_ref[...]
-    for d in range(6):
-        arrived_out[:, d, :] = moved_ref[d, 0:22, :]
-        codes_out[:, d, :] = moved_ref[d, 22:26, :].astype(jnp.int32) - 1
-
-    cells_x, cells_y, cells_z = pressure_ref.shape
-    row = lax.broadcasted_iota(jnp.int32, (cells_y, cells_z), 0)
-    lane = lax.broadcasted_iota(jnp.int32, (cells_y, cells_z), 1)
-    for x in range(cells_x):
-        here = pressure_ref[x]
-        total = pressure_ref[x - 1] if x > 0 else face_x_ref[0]
-        total = total + (pressure_ref[x + 1] if x < cells_x - 1 else face_x_ref[1])
-        total = total + jnp.where(row == 0, face_y_ref[0, x : x + 1, :], pltpu.roll(here, 1, 0))
-        total = total + jnp.where(
-            row == cells_y - 1, face_y_ref[1, x : x + 1, :], pltpu.roll(here, cells_y - 1, 0)
-        )
-        total = total + jnp.where(
-            lane == 0,
-            jnp.broadcast_to(face_z_ref[0][:, x : x + 1], here.shape),
-            pltpu.roll(here, 1, 1),
-        )
-        total = total + jnp.where(
-            lane == cells_z - 1,
-            jnp.broadcast_to(face_z_ref[1][:, x : x + 1], here.shape),
-            pltpu.roll(here, cells_z - 1, 1),
-        )
-        pressure_out[x] = total + source_ref[x]
-
+    loads = [
+        pltpu.make_async_copy(source, target, load_sem.at[n])
+        for n, (source, target) in enumerate(
+            (
+                (state_hbm.at[3:6], speed_ref),
+                (gas_hbm, gas_ref),
+                (radii_hbm, radii_ref),
+                (cells_hbm, cells_ref),
+                (pressure_hbm, pressure_ref),
+                (source_hbm, source_ref),
+                (face_x_hbm, face_x_ref),
+                (face_y_hbm, face_y_ref),
+                (face_z_hbm, face_z_ref),
+                (moved_hbm, moved_ref),
+            )
+        )
+    ]
+    for load in loads:
+        load.start()
+    stores = [
+        pltpu.make_async_copy(source, target, store_sem.at[n])
+        for n, (source, target) in enumerate(
+            (
+                (state_hbm.at[0:3], pos_out),
+                (state_hbm.at[3:6], vel_out),
+                (state_hbm.at[6:9], spin_out),
+                (springs_hbm, springs_out),
+                (arrived_ref, arrived_out),
+                (codes_ref, codes_out),
+                (result_ref, pressure_out),
+            )
+        )
+    ]
+    stores += [
+        pltpu.make_async_copy(
+            force_ref.at[:, 8 * n : 8 * n + 8], force_out.at[:, 8 * n : 8 * n + 8], store_sem.at[7 + n]
+        )
+        for n in range(2)
+    ]
+    for store in stores[:4]:
+        store.start()
+
+    for load in loads[:4]:
+        load.wait()
+    size_x, size_y = pressure_ref.shape[0] // 2, pressure_ref.shape[1] // 2
     live = jnp.where(live_mask(counts_ref), 1.0, 0.0)
     radius = radii_ref[...]
-    values = [drag_coeff * (state_ref[3 + i] - gas_ref[i]) * live for i in range(3)]
+    values = [drag_coeff * (speed_ref[i] - gas_ref[i]) * live for i in range(3)]
     values.append(4.0 / 3.0 * math.pi * (radius * radius * radius) * live)
     values = [halves(value) for value in values]
-    size_x, size_y = cells_x // 2, cells_y // 2
     for b in range(BINS):
         bx, by, bz = b // 4, b // 2 % 2, b % 2
         block = (
@@ -569,10 +660,46 @@
             product[i * SLOTS : (i + 1) * SLOTS].reshape(size_x, size_y, SLOTS) for i in range(4)
         ]
         for i in range(3):
-            force_out[(i,) + block] = parts[i]
-        pressure_out[block] = (
-            pressure_out[block] + volume_coeff * parts[3] + drag_weight * parts[2]
-        ) / 6.0
+            force_ref[(i,) + block] = parts[i]
+        result_ref[block] = volume_coeff * parts[3] + drag_weight * parts[2]
+        if b % 4 == 3:
+            stores[7 + b // 4].start()
+
+    for load in loads[4:]:
+        load.wait()
+    cells_x, cells_y, cells_z = pressure_ref.shape
+    row = lax.broadcasted_iota(jnp.int32, (cells_y, cells_z), 0)
+    lane = lax.broadcasted_iota(jnp.int32, (cells_y, cells_z), 1)
+    for x in range(cells_x):
+        here = pressure_ref[x]
+        total = pressure_ref[x - 1] if x > 0 else face_x_ref[0]
+        total = total + (pressure_ref[x + 1] if x < cells_x - 1 else face_x_ref[1])
+        total = total + jnp.where(row == 0, face_y_ref[0, x : x + 1, :], pltpu.roll(here, 1, 0))
+        total = total + jnp.where(
+            row == cells_y - 1, face_y_ref[1, x : x + 1, :], pltpu.roll(here, cells_y - 1, 0)
+        )
+        total = total + jnp.where(
+            lane == 0,
+            jnp.broadcast_to(face_z_ref[0][:, x : x + 1], here.shape),
+            pltpu.roll(here, 1, 1),
+        )
+        total = total + jnp.where(
+            lane == cells_z - 1,
+            jnp.broadcast_to(face_z_ref[1][:, x : x + 1], here.shape),
+            pltpu.roll(here, cells_z - 1, 1),
+        )
+        result_ref[x] = (total + source_ref[x] + result_ref[x]) / 6.0
+
+    stores[6].start()
+
+    for d in range(6):
+        codes_ref[d] = moved_ref[d, 22:26, :].astype(jnp.int32) - 1
+        for f in range(22):
+            arrived_ref[f * 6 + d] = moved_ref[d, f : f + 1, :]
+    stores[4].start()
+    stores[5].start()
+    for store in stores:
+        store.wait()
 
 
 def body(
@@ -591,14 +718,12 @@
 ):
     cells_x, cells_y, cells_z = pressure.shape
     f32 = jnp.float32
-    vmem = pl.BlockSpec(memory_space=pltpu.VMEM)
     smem = pl.BlockSpec(memory_space=pltpu.SMEM)
-    anywhere = pl.BlockSpec(memory_space=pl.ANY)
+    far = pl.BlockSpec(memory_space=pltpu.HBM)
     shape = jax.ShapeDtypeStruct
     rows = (BINS, SLOTS)
     radii_rows = radii.reshape(rows)
     cells_rows = cells.reshape(rows)
-    counts_row = counts.reshape(BINS)
     state, new_springs, gas, moved, face_x, face_y, face_z = pl.pallas_call(
         particles,
         out_shape=(
@@ -610,14 +735,26 @@
             shape((2, cells_x, cells_z), f32),
             shape((2, cells_y, SLOTS), f32),
         ),
-        in_specs=[vmem] * 4 + [smem] + [vmem] * 4 + [anywhere] * 2,
-        out_specs=(vmem,) * 7,
+        in_specs=[smem] + [far] * 10,
+        out_specs=(far,) * 7,
         scratch_shapes=[
+            pltpu.VMEM((9,) + rows, f32),
+            pltpu.VMEM((3 * HIST,) + rows, f32),
+            pltpu.VMEM((3,) + rows, f32),
+            pltpu.VMEM((3,) + rows, f32),
+            pltpu.VMEM((3,) + rows, f32),
+            pltpu.VMEM((3,) + rows, f32),
+            pltpu.VMEM(rows, f32),
+            pltpu.VMEM((3 * HIST,) + rows, f32),
+            pltpu.VMEM((HIST,) + rows, jnp.int32),
+            pltpu.VMEM(rows, jnp.int32),
+            pltpu.VMEM((6, 1, SLOTS), jnp.int32),
             pltpu.VMEM(fluid_velocity.shape, f32),
             pltpu.VMEM(pressure.shape, f32),
             pltpu.VMEM((7, 10) + rows, f32),
             pltpu.VMEM((SLOTS, SLOTS), f32),
-            pltpu.VMEM((SLOTS, SLOTS), f32),
+            pltpu.VMEM((7, BINS, SLOTS, SLOTS), f32),
+            pltpu.VMEM((3, BINS, SLOTS, SLOTS), f32),
             pltpu.VMEM((10,) + rows, f32),
             pltpu.VMEM((6, 10) + rows, f32),
             pltpu.VMEM((9,) + rows, f32),
@@ -630,23 +767,24 @@
             pltpu.VMEM((2, cells_y, cells_z), f32),
             pltpu.VMEM((2, cells_x, cells_z), f32),
             pltpu.VMEM((2, cells_y, SLOTS), f32),
-            pltpu.SemaphoreType.DMA((2,)),
+            pltpu.SemaphoreType.DMA((10,)),
+            pltpu.SemaphoreType.DMA((7,)),
             pltpu.SemaphoreType.DMA((4, 6)),
             pltpu.SemaphoreType.DMA((4, 6)),
         ],
         compiler_params=pltpu.CompilerParams(
-            collective_id=0, has_side_effects=True, vmem_limit_bytes=32 * 1024 * 1024
+            collective_id=0, has_side_effects=True, vmem_limit_bytes=VMEM_LIMIT
         ),
     )(
+        counts,
         positions.reshape((3,) + rows),
         velocities.reshape((3,) + rows),
         spins.reshape((3,) + rows),
         radii_rows,
-        counts_row,
         springs.reshape((3 * HIST,) + rows),
         partners.reshape((HIST,) + rows),
         cells_rows,
-        departures.reshape(6, SLOTS),
+        departures.reshape(6, 1, SLOTS),
         fluid_velocity,
         pressure,
     )
@@ -659,18 +797,36 @@
             shape((3 * HIST,) + rows, f32),
             shape(fluid_velocity.shape, f32),
             shape(pressure.shape, f32),
-            shape((22, 6, SLOTS), f32),
-            shape((4, 6, SLOTS), jnp.int32),
+            shape((132, 1, SLOTS), f32),
+            shape((6, 4, SLOTS), jnp.int32),
         ),
-        in_specs=[vmem] * 4 + [smem] + [vmem] * 7,
-        out_specs=(vmem,) * 8,
-        compiler_params=pltpu.CompilerParams(vmem_limit_bytes=32 * 1024 * 1024),
+        in_specs=[smem] + [far] * 11,
+        out_specs=(far,) * 8,
+        scratch_shapes=[
+            pltpu.VMEM((3,) + rows, f32),
+            pltpu.VMEM((3,) + rows, f32),
+            pltpu.VMEM(rows, f32),
+            pltpu.VMEM(rows, jnp.int32),
+            pltpu.VMEM((6, 32, SLOTS), f32),
+            pltpu.VMEM(pressure.shape, f32),
+            pltpu.VMEM(pressure.shape, f32),
+            pltpu.VMEM((2, cells_y, cells_z), f32),
+            pltpu.VMEM((2, cells_x, cells_z), f32),
+            pltpu.VMEM((2, cells_y, SLOTS), f32),
+            pltpu.VMEM(fluid_velocity.shape, f32),
+            pltpu.VMEM(pressure.shape, f32),
+            pltpu.VMEM((132, 1, SLOTS), f32),
+            pltpu.VMEM((6, 4, SLOTS), jnp.int32),
+            pltpu.SemaphoreType.DMA((10,)),
+            pltpu.SemaphoreType.DMA((9,)),
+        ],
+        compiler_params=pltpu.CompilerParams(vmem_limit_bytes=VMEM_LIMIT),
     )(
+        counts,
         state,
         new_springs,
         gas,
         radii_rows,
-        counts_row,
         cells_rows,
         moved,
         pressure,
@@ -686,8 +842,8 @@
         last_springs.reshape(springs.shape),
         force,
         new_pressure,
-        arrived[None, None, None],
-        codes[None, None, None],
+        arrived.reshape(1, 1, 1, 22, 6, SLOTS),
+        jnp.swapaxes(codes, 0, 1)[None, None, None],
     )
 
 

time: 61 us -> 30.3 us (0.50)
  Pallas kernels: 49.6 us -> 29.3 us
  local copies, waits for them, and re-layouts: 10.2 us -> 0 us
    pallas_call x1, Pallas kernels: 46.9 us -> 24.7 us  [body(): pl.pallas_call(particles, out_shape=(shape((9,) + rows, f32), shape((3 *...]
    unnamed x23 -> x0, local copies, waits for them, and re-layouts: 9.45 us -> none
    pallas_call x1, Pallas kernels: 2.7 us -> 4.6 us  [body(): pl.pallas_call(finish, out_shape=(shape((3,) + rows, f32), shape((3,) + r...]
    reshape x1 -> x0, local copies, waits for them, and re-layouts: 0.76 us -> none  [body(): counts_row = counts.reshape(BINS)]
where the time goes in v1:
time: 30.3 us; the launch traced here: 30 us
  Pallas kernels  29.3 us (97%)
  between operations  0.64 us (2%)
    pallas_call x1, Pallas kernels, body(): pl.pallas_call(particles, out_shape=(shape((9,) + rows, f32), shape((3 *...  24.7 us
    pallas_call x1, Pallas kernels, body(): pl.pallas_call(finish, out_shape=(shape((3,) + rows, f32), shape((3,) + r...  4.6 us

profile of v1, /device:TPU:1, one launch (start us, length us, event | category | flops | bytes accessed | tf_op | source)
XLA Modules:
  0.0 30.0 jit_solution(11679684990542424084)
XLA Ops:
  0.6 24.7 %shard_map.179 = (f32[9,8,128]{2,1,0:T(8,128)}, f32[12,8,128]{2,1,0:T(8,128)}, f32[3,8,128]{2,1,0:T(8,128)}, f32[6,32,128]{2,1,0:T(8,128)}, f32[2,32,256]{2,1,0:...) custom-call(s32[2,2,2]{2,1,0:T(2,128)} %counts_ref.3, f32[3,8,128]{2,1,0:T(8,128)} %bitcast.24, ...), custom_call_target="tpu_custom_call" | custom-call | tf_op jit(solution)/shard_map/pallas_call | solution.py:727
  25.4 4.6 %shard_map.180 = (f32[3,8,128]{2,1,0:T(8,128)}, f32[3,8,128]{2,1,0:T(8,128)}, f32[3,8,128]{2,1,0:T(8,128)}, f32[12,8,128]{2,1,0:T(8,128)}, f32[3,16,32,256]{3,2,...) custom-call(s32[2,2,2]{2,1,0:T(2,128)} %counts_ref.3, ...), custom_call_target="tpu_custom_call" | custom-call | tf_op jit(solution)/shard_map/pallas_call | solution.py:791

commit v2 on v1

--- a/solution.py
+++ b/solution.py
@@ -162,13 +162,15 @@
     departures_hbm,
     gas_hbm,
     pressure_hbm,
-    state_hbm,
-    new_springs_hbm,
-    u_hbm,
-    moved_hbm,
-    face_x_hbm,
-    face_y_hbm,
-    face_z_hbm,
+    source_hbm,
+    places_out,
+    speeds_out,
+    turning_out,
+    new_springs_out,
+    force_out,
+    result_out,
+    arrived_out,
+    codes_out,
     state_out,
     springs_out,
     gas_out,
@@ -182,6 +184,11 @@
     departures_ref,
     gas_ref,
     pressure_ref,
+    source_ref,
+    force_ref,
+    result_ref,
+    arrived_ref,
+    codes_ref,
     table_ref,
     columns_ref,
     mine_ref,
@@ -217,6 +224,7 @@
                 (cells_hbm, cells_ref),
                 (departures_hbm, departures_ref),
                 (gas_hbm, gas_ref),
+                (source_hbm, source_ref),
             )
         )
     ]
@@ -302,14 +310,6 @@
             face = (face_x_ref, face_y_ref, face_z_ref)[s // 2]
             face[s % 2] = jnp.zeros(face.shape[1:], jnp.float32)
 
-    pl.semaphore_wait(barrier, sum(there[d][1].astype(jnp.int32) for d in range(6)))
-
-    for d in range(6):
-
-        @pl.when(there[d][1])
-        def _():
-            halo_copy(d).start()
-
     for load in loads[4:9]:
         load.wait()
     cells_x, cells_y, cells_z = pressure_ref.shape
@@ -324,12 +324,6 @@
                 column = pressure_ref[x, :, cells_z - SLOTS : cells_z][:, SLOTS - 1 : SLOTS]
             face = jnp.where(lane == x, jnp.broadcast_to(column, (cells_y, SLOTS)), face)
         send_z_ref[side] = face
-    for d in range(6):
-
-        @pl.when(there[d][1])
-        def _():
-            face_copy(d).start()
-
     bits = bin_bits()
     code = [partners_ref[k] for k in range(HIST)]
     valid = [jnp.where(code[k] >= 0, 1.0, 0.0) for k in range(HIST)]
@@ -373,11 +367,27 @@
                     value = value + jnp.where(bits[axis] == 0, -1.0, 1.0)
                 table_ref[4 + axis, f] = value
 
+    inner_tables([own_ref[f] for f in range(10)])
+    pl.semaphore_wait(barrier, sum(there[d][1].astype(jnp.int32) for d in range(6)))
+
+    for d in range(6):
+
+        @pl.when(there[d][1])
+        def _():
+            halo_copy(d).start()
+
+    for d in range(6):
+
+        @pl.when(there[d][1])
+        def _():
+            face_copy(d).start()
+
     zero = jnp.zeros((BINS, SLOTS), jnp.float32)
     for step in range(SUBSTEPS):
         source = own_ref if step == 0 else own_2_ref
         fields = [source[f] for f in range(9)] + [partner_radius]
-        inner_tables(fields)
+        if step > 0:
+            inner_tables(fields)
         pair_pass(columns_ref, mine_ref, table_ref, (0, 1, 2, 3), sums_ref, True)
 
         if step == 0:
@@ -478,17 +488,18 @@
         pltpu.make_async_copy(source, target, store_sem.at[n])
         for n, (source, target) in enumerate(
             (
-                (state_out, state_hbm),
-                (springs_out, new_springs_hbm),
-                (gas_out, u_hbm),
-                (face_x_ref, face_x_hbm),
-                (face_y_ref, face_y_hbm),
-                (face_z_ref, face_z_hbm),
-                (come_ref, moved_hbm),
+                (state_out.at[0:3], places_out),
+                (state_out.at[3:6], speeds_out),
+                (state_out.at[6:9], turning_out),
+                (springs_out, new_springs_out),
+                (force_ref, force_out),
+                (result_ref, result_out),
+                (arrived_ref, arrived_out),
+                (codes_ref, codes_out),
             )
         )
     ]
-    for store in stores[:3]:
+    for store in stores[:4]:
         store.start()
 
     for f in range(9):
@@ -517,6 +528,8 @@
         def _():
             moved_copy(d).start()
 
+    deposit(counts_ref, radii_ref, cells_ref, state_out, gas_out, force_ref, result_ref)
+    stores[4].start()
     for d in range(6):
 
         @pl.when(there[d][1])
@@ -526,9 +539,9 @@
             face_copy(d).wait_send()
             face_copy(d ^ 1).wait_recv()
 
-    for store in stores[3:6]:
-        store.start()
-
+    loads[10].wait()
+    sweep(pressure_ref, source_ref, face_x_ref, face_y_ref, face_z_ref, result_ref)
+    stores[5].start()
     for d in range(6):
 
         @pl.when(there[d][1])
@@ -536,97 +549,21 @@
             moved_copy(d).wait_send()
             moved_copy(d ^ 1).wait_recv()
 
-    stores[6].start()
+    for d in range(6):
+        codes_ref[d] = come_ref[d, 22:26, :].astype(jnp.int32) - 1
+        for f in range(22):
+            arrived_ref[f * 6 + d] = come_ref[d, f : f + 1, :]
+    for store in stores[6:]:
+        store.start()
     for store in stores:
         store.wait()
 
 
-def finish(
-    counts_ref,
-    state_hbm,
-    springs_hbm,
-    gas_hbm,
-    radii_hbm,
-    cells_hbm,
-    moved_hbm,
-    pressure_hbm,
-    source_hbm,
-    face_x_hbm,
-    face_y_hbm,
-    face_z_hbm,
-    pos_out,
-    vel_out,
-    spin_out,
-    springs_out,
-    force_out,
-    pressure_out,
-    arrived_out,
-    codes_out,
-    speed_ref,
-    gas_ref,
-    radii_ref,
-    cells_ref,
-    moved_ref,
-    pressure_ref,
-    source_ref,
-    face_x_ref,
-    face_y_ref,
-    face_z_ref,
-    force_ref,
-    result_ref,
-    arrived_ref,
-    codes_ref,
-    load_sem,
-    store_sem,
-):
-    loads = [
-        pltpu.make_async_copy(source, target, load_sem.at[n])
-        for n, (source, target) in enumerate(
-            (
-                (state_hbm.at[3:6], speed_ref),
-                (gas_hbm, gas_ref),
-                (radii_hbm, radii_ref),
-                (cells_hbm, cells_ref),
-                (pressure_hbm, pressure_ref),
-                (source_hbm, source_ref),
-                (face_x_hbm, face_x_ref),
-                (face_y_hbm, face_y_ref),
-                (face_z_hbm, face_z_ref),
-                (moved_hbm, moved_ref),
-            )
-        )
-    ]
-    for load in loads:
-        load.start()
-    stores = [
-        pltpu.make_async_copy(source, target, store_sem.at[n])
-        for n, (source, target) in enumerate(
-            (
-                (state_hbm.at[0:3], pos_out),
-                (state_hbm.at[3:6], vel_out),
-                (state_hbm.at[6:9], spin_out),
-                (springs_hbm, springs_out),
-                (arrived_ref, arrived_out),
-                (codes_ref, codes_out),
-                (result_ref, pressure_out),
-            )
-        )
-    ]
-    stores += [
-        pltpu.make_async_copy(
-            force_ref.at[:, 8 * n : 8 * n + 8], force_out.at[:, 8 * n : 8 * n + 8], store_sem.at[7 + n]
-        )
-        for n in range(2)
-    ]
-    for store in stores[:4]:
-        store.start()
-
-    for load in loads[:4]:
-        load.wait()
-    size_x, size_y = pressure_ref.shape[0] // 2, pressure_ref.shape[1] // 2
+def deposit(counts_ref, radii_ref, cells_ref, state_ref, gas_ref, force_ref, result_ref):
+    size_x, size_y = result_ref.shape[0] // 2, result_ref.shape[1] // 2
     live = jnp.where(live_mask(counts_ref), 1.0, 0.0)
     radius = radii_ref[...]
-    values = [drag_coeff * (speed_ref[i] - gas_ref[i]) * live for i in range(3)]
+    values = [drag_coeff * (state_ref[3 + i] - gas_ref[i]) * live for i in range(3)]
     values.append(4.0 / 3.0 * math.pi * (radius * radius * radius) * live)
     values = [halves(value) for value in values]
     for b in range(BINS):
@@ -662,11 +599,9 @@
         for i in range(3):
             force_ref[(i,) + block] = parts[i]
         result_ref[block] = volume_coeff * parts[3] + drag_weight * parts[2]
-        if b % 4 == 3:
-            stores[7 + b // 4].start()
-
-    for load in loads[4:]:
-        load.wait()
+
+
+def sweep(pressure_ref, source_ref, face_x_ref, face_y_ref, face_z_ref, result_ref):
     cells_x, cells_y, cells_z = pressure_ref.shape
     row = lax.broadcasted_iota(jnp.int32, (cells_y, cells_z), 0)
     lane = lax.broadcasted_iota(jnp.int32, (cells_y, cells_z), 1)
@@ -690,14 +625,25 @@
         )
         result_ref[x] = (total + source_ref[x] + result_ref[x]) / 6.0
 
-    stores[6].start()
-
-    for d in range(6):
-        codes_ref[d] = moved_ref[d, 22:26, :].astype(jnp.int32) - 1
-        for f in range(22):
-            arrived_ref[f * 6 + d] = moved_ref[d, f : f + 1, :]
-    stores[4].start()
-    stores[5].start()
+
+def finish(*refs):
+    sources, targets, held = refs[0:8], refs[8:16], refs[16:24]
+    load_sem, store_sem = refs[24:26]
+    parts = [(4, i) for i in range(3)] + [(n, None) for n in (5, 3, 6, 0, 1, 2, 7)]
+
+    def piece(ref, part):
+        return ref if part is None else ref.at[part]
+
+    loads, stores = [], []
+    for m, (n, part) in enumerate(parts):
+        middle = piece(held[n], part)
+        loads.append(pltpu.make_async_copy(piece(sources[n], part), middle, load_sem.at[m]))
+        stores.append(pltpu.make_async_copy(middle, piece(targets[n], part), store_sem.at[m]))
+    for load in loads:
+        load.start()
+    for load, store in zip(loads, stores):
+        load.wait()
+        store.start()
     for store in stores:
         store.wait()
 
@@ -722,21 +668,21 @@
     far = pl.BlockSpec(memory_space=pltpu.HBM)
     shape = jax.ShapeDtypeStruct
     rows = (BINS, SLOTS)
-    radii_rows = radii.reshape(rows)
-    cells_rows = cells.reshape(rows)
-    state, new_springs, gas, moved, face_x, face_y, face_z = pl.pallas_call(
+    results = (
+        shape((3,) + rows, f32),
+        shape((3,) + rows, f32),
+        shape((3,) + rows, f32),
+        shape((3 * HIST,) + rows, f32),
+        shape(fluid_velocity.shape, f32),
+        shape(pressure.shape, f32),
+        shape((132, 1, SLOTS), f32),
+        shape((6, 4, SLOTS), jnp.int32),
+    )
+    made = pl.pallas_call(
         particles,
-        out_shape=(
-            shape((9,) + rows, f32),
-            shape((3 * HIST,) + rows, f32),
-            shape((3,) + rows, f32),
-            shape((6, 32, SLOTS), f32),
-            shape((2, cells_y, cells_z), f32),
-            shape((2, cells_x, cells_z), f32),
-            shape((2, cells_y, SLOTS), f32),
-        ),
-        in_specs=[smem] + [far] * 10,
-        out_specs=(far,) * 7,
+        out_shape=results,
+        in_specs=[smem] + [far] * 11,
+        out_specs=(far,) * 8,
         scratch_shapes=[
             pltpu.VMEM((9,) + rows, f32),
             pltpu.VMEM((3 * HIST,) + rows, f32),
@@ -751,6 +697,11 @@
             pltpu.VMEM((6, 1, SLOTS), jnp.int32),
             pltpu.VMEM(fluid_velocity.shape, f32),
             pltpu.VMEM(pressure.shape, f32),
+            pltpu.VMEM(pressure.shape, f32),
+            pltpu.VMEM(fluid_velocity.shape, f32),
+            pltpu.VMEM(pressure.shape, f32),
+            pltpu.VMEM((132, 1, SLOTS), f32),
+            pltpu.VMEM((6, 4, SLOTS), jnp.int32),
             pltpu.VMEM((7, 10) + rows, f32),
             pltpu.VMEM((SLOTS, SLOTS), f32),
             pltpu.VMEM((7, BINS, SLOTS, SLOTS), f32),
@@ -767,8 +718,8 @@
             pltpu.VMEM((2, cells_y, cells_z), f32),
             pltpu.VMEM((2, cells_x, cells_z), f32),
             pltpu.VMEM((2, cells_y, SLOTS), f32),
-            pltpu.SemaphoreType.DMA((10,)),
-            pltpu.SemaphoreType.DMA((7,)),
+            pltpu.SemaphoreType.DMA((11,)),
+            pltpu.SemaphoreType.DMA((9,)),
             pltpu.SemaphoreType.DMA((4, 6)),
             pltpu.SemaphoreType.DMA((4, 6)),
         ],
@@ -780,61 +731,24 @@
         positions.reshape((3,) + rows),
         velocities.reshape((3,) + rows),
         spins.reshape((3,) + rows),
-        radii_rows,
+        radii.reshape(rows),
         springs.reshape((3 * HIST,) + rows),
         partners.reshape((HIST,) + rows),
-        cells_rows,
+        cells.reshape(rows),
         departures.reshape(6, 1, SLOTS),
         fluid_velocity,
         pressure,
+        pressure_source,
     )
     places, speeds, turning, last_springs, force, new_pressure, arrived, codes = pl.pallas_call(
         finish,
-        out_shape=(
-            shape((3,) + rows, f32),
-            shape((3,) + rows, f32),
-            shape((3,) + rows, f32),
-            shape((3 * HIST,) + rows, f32),
-            shape(fluid_velocity.shape, f32),
-            shape(pressure.shape, f32),
-            shape((132, 1, SLOTS), f32),
-            shape((6, 4, SLOTS), jnp.int32),
-        ),
-        in_specs=[smem] + [far] * 11,
+        out_shape=results,
+        in_specs=[far] * 8,
         out_specs=(far,) * 8,
-        scratch_shapes=[
-            pltpu.VMEM((3,) + rows, f32),
-            pltpu.VMEM((3,) + rows, f32),
-            pltpu.VMEM(rows, f32),
-            pltpu.VMEM(rows, jnp.int32),
-            pltpu.VMEM((6, 32, SLOTS), f32),
-            pltpu.VMEM(pressure.shape, f32),
-            pltpu.VMEM(pressure.shape, f32),
-            pltpu.VMEM((2, cells_y, cells_z), f32),
-            pltpu.VMEM((2, cells_x, cells_z), f32),
-            pltpu.VMEM((2, cells_y, SLOTS), f32),
-            pltpu.VMEM(fluid_velocity.shape, f32),
-            pltpu.VMEM(pressure.shape, f32),
-            pltpu.VMEM((132, 1, SLOTS), f32),
-            pltpu.VMEM((6, 4, SLOTS), jnp.int32),
-            pltpu.SemaphoreType.DMA((10,)),
-            pltpu.SemaphoreType.DMA((9,)),
-        ],
+        scratch_shapes=[pltpu.VMEM(result.shape, result.dtype) for result in results]
+        + [pltpu.SemaphoreType.DMA((10,)), pltpu.SemaphoreType.DMA((10,))],
         compiler_params=pltpu.CompilerParams(vmem_limit_bytes=VMEM_LIMIT),
-    )(
-        counts,
-        state,
-        new_springs,
-        gas,
-        radii_rows,
-        cells_rows,
-        moved,
-        pressure,
-        pressure_source,
-        face_x,
-        face_y,
-        face_z,
-    )
+    )(*made)
     return (
         places.reshape(positions.shape),
         speeds.reshape(positions.shape),

time: 30.3 us -> 27.8 us (0.917)
  Pallas kernels: 29.3 us -> 27 us
    pallas_call x2, Pallas kernels: 29.3 us -> 27 us  [the longest x1 24.4 us: body(): pl.pallas_call(particles, out_shape=results, in_specs=[smem] + [far] * 11...]
where the time goes in v2:
time: 27.8 us; the launch traced here: 27.7 us
  Pallas kernels  27 us (97%)
  between operations  0.65 us (2%)
    pallas_call x1, Pallas kernels, body(): pl.pallas_call(particles, out_shape=results, in_specs=[smem] + [far] * 11...  24.4 us
    pallas_call x1, Pallas kernels, body(): pl.pallas_call(finish, out_shape=results, in_specs=[far] * 8, out_specs=(...  2.56 us

profile of v2, /device:TPU:1, one launch (start us, length us, event | category | flops | bytes accessed | tf_op | source)
XLA Modules:
  0.0 27.7 jit_solution(17386468357405409515)
XLA Ops:
  0.6 24.4 %shard_map.179 = (f32[3,8,128]{2,1,0:T(8,128)}, f32[3,8,128]{2,1,0:T(8,128)}, f32[3,8,128]{2,1,0:T(8,128)}, f32[12,8,128]{2,1,0:T(8,128)}, f32[3,16,32,256]{3,2,...) custom-call(s32[2,2,2]{2,1,0:T(2,128)} %counts_ref.1, f32[3,8,128]{2,1,0:T(8,128)} %bitcast.20, ...), custom_call_target="tpu_custom_call" | custom-call | tf_op jit(solution)/shard_map/pallas_call | solution.py:681
  25.1 2.6 %shard_map.180 = (f32[3,8,128]{2,1,0:T(8,128)}, f32[3,8,128]{2,1,0:T(8,128)}, f32[3,8,128]{2,1,0:T(8,128)}, f32[12,8,128]{2,1,0:T(8,128)}, f32[3,16,32,256]{3,2,...) custom-call(f32[3,8,128]{2,1,0:T(8,128)} %get-tuple-element.24.refs_0_, ...), custom_call_target="tpu_custom_call" | custom-call | tf_op jit(solution)/shard_map/pallas_call | solution.py:743

commit v3 on v2

--- a/solution.py
+++ b/solution.py
@@ -28,6 +28,7 @@
 
 NOBODY = -10.0
 TINY = 1e-30
+SPEED_SCALE = normal_damp / normal_stiff
 AXES = ("gx", "gy", "gz")
 MESH = pl.DeviceIdType.MESH
 
@@ -85,44 +86,62 @@
     return a[0] * b[0] + a[1] * b[1] + a[2] * b[2]
 
 
-def pair_pass(columns_ref, mine_ref, table_ref, tables, sums_ref, first):
-    def chunk(c, carry):
-        start = pl.multiple_of(c * 8, 8)
-        rows = pl.ds(start, 8)
-        tile = columns_ref[rows, :] if first else None
-        for b in range(BINS):
-            if first:
-                mine = [
-                    jnp.broadcast_to(tile[:, f * 8 + b : f * 8 + b + 1], (8, SLOTS))
-                    for f in range(7)
-                ]
-                for f in range(7):
-                    mine_ref[f, b, rows, :] = mine[f]
-                total = None
-            else:
-                mine = [mine_ref[f, b, rows, :] for f in range(7)]
-                total = [sums_ref[i, b, rows, :] for i in range(3)]
-            for t in tables:
-                other = [
-                    jnp.broadcast_to(table_ref[t, f, b : b + 1, :], (8, SLOTS))
-                    for f in (0, 1, 2, 3, 4, 5, 9)
-                ]
-                sep = [mine[i] - other[i] for i in range(3)]
-                square = dot(sep, sep) + soft_length**2
-                inverse = lax.rsqrt(square)
-                overlap = mine[6] + other[6] - square * inverse
-                delta = jnp.maximum(overlap, 0.0)
-                root = delta * lax.rsqrt(jnp.maximum(overlap, TINY))
-                vrel = [mine[3 + i] - other[3 + i] for i in range(3)]
-                approach = dot(vrel, sep) * inverse
-                weight = ((normal_stiff / normal_damp) * delta - approach) * (root * inverse)
-                term = [weight * sep[i] for i in range(3)]
-                total = term if total is None else [total[i] + term[i] for i in range(3)]
-            for i in range(3):
-                sums_ref[i, b, rows, :] = total[i]
+def spread(table_ref, radii_ref, mine_ref, b):
+    for f in range(7):
+        row = radii_ref[b : b + 1, :] if f == 6 else table_ref[0, f, b : b + 1, :]
+        if f in (3, 4, 5):
+            row = row * SPEED_SCALE
+        mine_ref[f, b] = jnp.broadcast_to(row, (SLOTS, SLOTS)).T
+
+
+def bin_pairs(mine_ref, table_ref, scaled_ref, tables, sums_ref, first, b):
+    row = pl.ds(b, 1)
+    for c in range(SLOTS // 8):
+        rows = slice(c * 8, c * 8 + 8)
+        mine = [mine_ref[f, b, rows, :] for f in range(7)]
+        total = None if first else [sums_ref[i, b, rows, :] for i in range(3)]
+        for t in tables:
+            other = [
+                jnp.broadcast_to(ref[t, f, row, :], (8, SLOTS))
+                for ref, f in (
+                    (table_ref, 0),
+                    (table_ref, 1),
+                    (table_ref, 2),
+                    (scaled_ref, 0),
+                    (scaled_ref, 1),
+                    (scaled_ref, 2),
+                    (table_ref, 9),
+                )
+            ]
+            sep = [mine[i] - other[i] for i in range(3)]
+            square = dot(sep, sep) + soft_length**2
+            inverse = lax.rsqrt(square)
+            overlap = mine[6] + other[6] - square * inverse
+            delta = jnp.maximum(overlap, 0.0)
+            root = delta * lax.rsqrt(jnp.maximum(overlap, TINY))
+            vrel = [mine[3 + i] - other[3 + i] for i in range(3)]
+            approach = dot(vrel, sep) * inverse
+            weight = (delta - approach) * (root * inverse)
+            term = [weight * sep[i] for i in range(3)]
+            total = term if total is None else [total[i] + term[i] for i in range(3)]
+        for i in range(3):
+            sums_ref[i, b, rows, :] = total[i]
+
+
+def inner_pairs(radii_ref, mine_ref, table_ref, scaled_ref, sums_ref):
+    spread(table_ref, radii_ref, mine_ref, 0)
+    for b in range(BINS):
+        if b < BINS - 1:
+            spread(table_ref, radii_ref, mine_ref, b + 1)
+        bin_pairs(mine_ref, table_ref, scaled_ref, (0, 1, 2, 3), sums_ref, True, b)
+
+
+def outer_pairs(mine_ref, table_ref, scaled_ref, sums_ref):
+    def one(b, carry):
+        bin_pairs(mine_ref, table_ref, scaled_ref, (4, 5, 6), sums_ref, False, b)
         return carry
 
-    lax.fori_loop(0, SLOTS // 8, chunk, 0)
+    lax.fori_loop(0, BINS, one, 0)
 
 
 def lane_sums(sums_ref, i):
@@ -190,7 +209,7 @@
     arrived_ref,
     codes_ref,
     table_ref,
-    columns_ref,
+    scaled_ref,
     mine_ref,
     sums_ref,
     own_ref,
@@ -351,9 +370,9 @@
                 if f == axis:
                     value = value + jnp.where(bits[axis] == 0, 1.0, -1.0)
                 table_ref[1 + axis, f] = value
-        columns_ref[...] = jnp.concatenate(
-            [fields[f] for f in range(6)] + [radius, jnp.zeros((72, SLOTS), jnp.float32)], axis=0
-        ).T
+        for t in range(4):
+            for i in range(3):
+                scaled_ref[t, i] = table_ref[t, 3 + i] * SPEED_SCALE
 
     def outer_tables(ref, count):
         for axis in range(3):
@@ -366,6 +385,8 @@
                 if f == axis:
                     value = value + jnp.where(bits[axis] == 0, -1.0, 1.0)
                 table_ref[4 + axis, f] = value
+                if f in (3, 4, 5):
+                    scaled_ref[4 + axis, f - 3] = value * SPEED_SCALE
 
     inner_tables([own_ref[f] for f in range(10)])
     pl.semaphore_wait(barrier, sum(there[d][1].astype(jnp.int32) for d in range(6)))
@@ -388,7 +409,7 @@
         fields = [source[f] for f in range(9)] + [partner_radius]
         if step > 0:
             inner_tables(fields)
-        pair_pass(columns_ref, mine_ref, table_ref, (0, 1, 2, 3), sums_ref, True)
+        inner_pairs(radii_ref, mine_ref, table_ref, scaled_ref, sums_ref)
 
         if step == 0:
             loads[9].wait()
@@ -424,7 +445,7 @@
                 (halo_copy if step == 0 else halo_copy_2)(d ^ 1).wait_recv()
 
         outer_tables(halo_ref if step == 0 else halo_2_ref, 10 if step == 0 else 9)
-        pair_pass(columns_ref, mine_ref, table_ref, (4, 5, 6), sums_ref, False)
+        outer_pairs(mine_ref, table_ref, scaled_ref, sums_ref)
         normal = [lane_sums(sums_ref, i) for i in range(3)]
 
         places, speeds, turning = fields[0:3], fields[3:6], fields[6:9]
@@ -469,7 +490,7 @@
             torque_sum = [torque_sum[i] + twist[i] for i in range(3)]
 
         for i in range(3):
-            push = normal_damp * normal[i] + shear_sum[i]
+            push = normal_stiff * normal[i] + shear_sum[i]
             push = push + drag_coeff * (gas_out[i] - speeds[i])
             speed = speeds[i] + time_step * (push / mass - (gravity if i == 2 else 0.0))
             spin = turning[i] + time_step * (radius * torque_sum[i]) / inertia
@@ -703,7 +724,7 @@
             pltpu.VMEM((132, 1, SLOTS), f32),
             pltpu.VMEM((6, 4, SLOTS), jnp.int32),
             pltpu.VMEM((7, 10) + rows, f32),
-            pltpu.VMEM((SLOTS, SLOTS), f32),
+            pltpu.VMEM((7, 3) + rows, f32),
             pltpu.VMEM((7, BINS, SLOTS, SLOTS), f32),
             pltpu.VMEM((3, BINS, SLOTS, SLOTS), f32),
             pltpu.VMEM((10,) + rows, f32),

time: 27.8 us -> 27 us (0.971)
  Pallas kernels: 27 us -> 26.2 us
    pallas_call x1, Pallas kernels: 24.4 us -> 23.6 us  [body(): pl.pallas_call(particles, out_shape=results, in_specs=[smem] + [far] * 11...]
where the time goes in v3:
time: 27 us; the launch traced here: 26.8 us
  Pallas kernels  26.2 us (97%)
  between operations  0.65 us (2%)
    pallas_call x1, Pallas kernels, body(): pl.pallas_call(particles, out_shape=results, in_specs=[smem] + [far] * 11...  23.6 us
    pallas_call x1, Pallas kernels, body(): pl.pallas_call(finish, out_shape=results, in_specs=[far] * 8, out_specs=(...  2.56 us

profile of v3, /device:TPU:1, one launch (start us, length us, event | category | flops | bytes accessed | tf_op | source)
XLA Modules:
  0.0 26.8 jit_solution(9551439936642731181)
XLA Ops:
  0.6 23.6 %shard_map.179 = (f32[3,8,128]{2,1,0:T(8,128)}, f32[3,8,128]{2,1,0:T(8,128)}, f32[3,8,128]{2,1,0:T(8,128)}, f32[12,8,128]{2,1,0:T(8,128)}, f32[3,16,32,256]{3,2,...) custom-call(s32[2,2,2]{2,1,0:T(2,128)} %counts_ref.1, f32[3,8,128]{2,1,0:T(8,128)} %bitcast.20, ...), custom_call_target="tpu_custom_call" | custom-call | tf_op jit(solution)/shard_map/pallas_call | solution.py:702
  24.3 2.6 %shard_map.180 = (f32[3,8,128]{2,1,0:T(8,128)}, f32[3,8,128]{2,1,0:T(8,128)}, f32[3,8,128]{2,1,0:T(8,128)}, f32[12,8,128]{2,1,0:T(8,128)}, f32[3,16,32,256]{3,2,...) custom-call(f32[3,8,128]{2,1,0:T(8,128)} %get-tuple-element.24.refs_0_, ...), custom_call_target="tpu_custom_call" | custom-call | tf_op jit(solution)/shard_map/pallas_call | solution.py:764

commit v4 on v3

--- a/solution.py
+++ b/solution.py
@@ -170,7 +170,7 @@
 
 
 def particles(
-    counts_ref,
+    counts_hbm,
     pos_hbm,
     vel_hbm,
     spin_hbm,
@@ -193,6 +193,7 @@
     state_out,
     springs_out,
     gas_out,
+    counts_ref,
     pos_ref,
     vel_ref,
     spin_ref,
@@ -213,9 +214,9 @@
     mine_ref,
     sums_ref,
     own_ref,
+    own_2_ref,
+    packed_ref,
     halo_ref,
-    own_2_ref,
-    halo_2_ref,
     picked_ref,
     gone_ref,
     come_ref,
@@ -237,6 +238,7 @@
                 (vel_hbm, vel_ref),
                 (spin_hbm, spin_ref),
                 (radii_hbm, radii_ref),
+                (counts_hbm, counts_ref),
                 (pressure_hbm, pressure_ref),
                 (partners_hbm, partners_ref),
                 (springs_hbm, springs_ref),
@@ -259,22 +261,12 @@
         def _():
             pl.semaphore_signal(barrier, inc=1, device_id=there[d][0], device_id_type=MESH)
 
-    def halo_copy(d):
+    def halo_copy(step, d):
         return pltpu.make_async_remote_copy(
-            src_ref=own_ref,
-            dst_ref=halo_ref.at[d ^ 1],
-            send_sem=send_sem.at[0, d],
-            recv_sem=recv_sem.at[0, d ^ 1],
-            device_id=there[d][0],
-            device_id_type=MESH,
-        )
-
-    def halo_copy_2(d):
-        return pltpu.make_async_remote_copy(
-            src_ref=own_2_ref,
-            dst_ref=halo_2_ref.at[d ^ 1],
-            send_sem=send_sem.at[1, d],
-            recv_sem=recv_sem.at[1, d ^ 1],
+            src_ref=packed_ref.at[step, d],
+            dst_ref=halo_ref.at[step, d ^ 1],
+            send_sem=send_sem.at[step, d],
+            recv_sem=recv_sem.at[step, d ^ 1],
             device_id=there[d][0],
             device_id_type=MESH,
         )
@@ -307,7 +299,7 @@
             device_id_type=MESH,
         )
 
-    for load in loads[:4]:
+    for load in loads[:5]:
         load.wait()
     live = live_mask(counts_ref)
     radius = radii_ref[...]
@@ -316,34 +308,38 @@
         own_ref[i] = pos_ref[i]
         own_ref[3 + i] = vel_ref[i]
         own_ref[6 + i] = spin_ref[i]
-    own_ref[9] = partner_radius
+    bits = bin_bits()
+
+    def send_halo(step, fields):
+        for d in range(6):
+            axis = d // 2
+            for n in range(5):
+                packed_ref[step, d, n] = jnp.where(
+                    bits[axis] == d % 2, fields[2 * n], swapped(fields[2 * n + 1], axis)
+                )
+        if step == 0:
+            pl.semaphore_wait(barrier, sum(there[d][1].astype(jnp.int32) for d in range(6)))
+        for d in range(6):
+
+            @pl.when(there[d][1])
+            def _():
+                halo_copy(step, d).start()
+
 
     for s in range(6):
 
         @pl.when(jnp.logical_not(there[s][1]))
         def _():
-            halo_ref[s] = jnp.zeros((10, BINS, SLOTS), jnp.float32)
-            halo_ref[s, 9] = jnp.full((BINS, SLOTS), NOBODY, jnp.float32)
-            halo_2_ref[s] = jnp.zeros((9, BINS, SLOTS), jnp.float32)
+            for step in range(SUBSTEPS):
+                halo_ref[step, s] = jnp.zeros((5, BINS, SLOTS), jnp.float32)
+                halo_ref[step, s, 4] = jnp.full((BINS, SLOTS), NOBODY, jnp.float32)
             come_ref[s ^ 1] = jnp.zeros((32, SLOTS), jnp.float32)
             face = (face_x_ref, face_y_ref, face_z_ref)[s // 2]
             face[s % 2] = jnp.zeros(face.shape[1:], jnp.float32)
 
-    for load in loads[4:9]:
+    send_halo(0, [own_ref[f] for f in range(9)] + [partner_radius])
+    for load in loads[5:10]:
         load.wait()
-    cells_x, cells_y, cells_z = pressure_ref.shape
-    lane = lax.broadcasted_iota(jnp.int32, (cells_y, SLOTS), 1)
-    for side in range(2):
-        send_y_ref[side] = pressure_ref[:, 0 if side == 0 else cells_y - 1, :]
-        face = jnp.zeros((cells_y, SLOTS), jnp.float32)
-        for x in range(cells_x):
-            if side == 0:
-                column = pressure_ref[x, :, 0:SLOTS][:, 0:1]
-            else:
-                column = pressure_ref[x, :, cells_z - SLOTS : cells_z][:, SLOTS - 1 : SLOTS]
-            face = jnp.where(lane == x, jnp.broadcast_to(column, (cells_y, SLOTS)), face)
-        send_z_ref[side] = face
-    bits = bin_bits()
     code = [partners_ref[k] for k in range(HIST)]
     valid = [jnp.where(code[k] >= 0, 1.0, 0.0) for k in range(HIST)]
     member = [jnp.maximum(code[k], 0) & (SLOTS - 1) for k in range(HIST)]
@@ -374,45 +370,49 @@
             for i in range(3):
                 scaled_ref[t, i] = table_ref[t, 3 + i] * SPEED_SCALE
 
-    def outer_tables(ref, count):
+    def outer_tables(step):
         for axis in range(3):
-            for f in range(count):
-                value = jnp.where(
-                    bits[axis] == 0,
-                    swapped(ref[2 * axis, f], axis),
-                    swapped(ref[2 * axis + 1, f], axis),
-                )
-                if f == axis:
-                    value = value + jnp.where(bits[axis] == 0, -1.0, 1.0)
-                table_ref[4 + axis, f] = value
-                if f in (3, 4, 5):
-                    scaled_ref[4 + axis, f - 3] = value * SPEED_SCALE
-
-    inner_tables([own_ref[f] for f in range(10)])
-    pl.semaphore_wait(barrier, sum(there[d][1].astype(jnp.int32) for d in range(6)))
-
-    for d in range(6):
-
-        @pl.when(there[d][1])
-        def _():
-            halo_copy(d).start()
-
-    for d in range(6):
-
-        @pl.when(there[d][1])
-        def _():
-            face_copy(d).start()
+            for n in range(5):
+                low, high = halo_ref[step, 2 * axis, n], halo_ref[step, 2 * axis + 1, n]
+                first = jnp.where(bits[axis] == 0, swapped(low, axis), swapped(high, axis))
+                second = jnp.where(bits[axis] == 0, low, high)
+                for f, value in ((2 * n, first), (2 * n + 1, second)):
+                    if f == axis:
+                        value = value + jnp.where(bits[axis] == 0, -1.0, 1.0)
+                    table_ref[4 + axis, f] = value
+                    if f in (3, 4, 5):
+                        scaled_ref[4 + axis, f - 3] = value * SPEED_SCALE
+
+    cells_x, cells_y, cells_z = pressure_ref.shape
+
+    def send_faces():
+        lane = lax.broadcasted_iota(jnp.int32, (cells_y, SLOTS), 1)
+        for side in range(2):
+            send_y_ref[side] = pressure_ref[:, 0 if side == 0 else cells_y - 1, :]
+            face = jnp.zeros((cells_y, SLOTS), jnp.float32)
+            for x in range(cells_x):
+                if side == 0:
+                    column = pressure_ref[x, :, 0:SLOTS][:, 0:1]
+                else:
+                    column = pressure_ref[x, :, cells_z - SLOTS : cells_z][:, SLOTS - 1 : SLOTS]
+                face = jnp.where(lane == x, jnp.broadcast_to(column, (cells_y, SLOTS)), face)
+            send_z_ref[side] = face
+        for d in range(6):
+
+            @pl.when(there[d][1])
+            def _():
+                face_copy(d).start()
 
     zero = jnp.zeros((BINS, SLOTS), jnp.float32)
     for step in range(SUBSTEPS):
         source = own_ref if step == 0 else own_2_ref
         fields = [source[f] for f in range(9)] + [partner_radius]
-        if step > 0:
-            inner_tables(fields)
+        inner_tables(fields)
         inner_pairs(radii_ref, mine_ref, table_ref, scaled_ref, sums_ref)
 
         if step == 0:
-            loads[9].wait()
+            send_faces()
+            loads[10].wait()
             for b in range(BINS):
                 bx, by, bz = b // 4, b // 2 % 2, b % 2
                 size_x, size_y = cells_x // 2, cells_y // 2
@@ -438,13 +438,23 @@
                         keepdims=True,
                     )
 
+        if step == 1:
+            for d in range(6):
+
+                @pl.when(there[d][1])
+                def _():
+                    face_copy(d ^ 1).wait_recv()
+
+            loads[11].wait()
+            sweep(pressure_ref, source_ref, face_x_ref, face_y_ref, face_z_ref, result_ref)
+
         for d in range(6):
 
             @pl.when(there[d][1])
             def _():
-                (halo_copy if step == 0 else halo_copy_2)(d ^ 1).wait_recv()
-
-        outer_tables(halo_ref if step == 0 else halo_2_ref, 10 if step == 0 else 9)
+                halo_copy(step, d ^ 1).wait_recv()
+
+        outer_tables(step)
         outer_pairs(mine_ref, table_ref, scaled_ref, sums_ref)
         normal = [lane_sums(sums_ref, i) for i in range(3)]
 
@@ -499,11 +509,7 @@
             target[6 + i] = spin
             target[i] = places[i] + time_step * speed
         if step == 0:
-            for d in range(6):
-
-                @pl.when(there[d][1])
-                def _():
-                    halo_copy_2(d).start()
+            send_halo(1, [own_2_ref[f] for f in range(9)] + [partner_radius])
 
     stores = [
         pltpu.make_async_copy(source, target, store_sem.at[n])
@@ -551,22 +557,14 @@
 
     deposit(counts_ref, radii_ref, cells_ref, state_out, gas_out, force_ref, result_ref)
     stores[4].start()
+    stores[5].start()
     for d in range(6):
 
         @pl.when(there[d][1])
         def _():
-            halo_copy(d).wait_send()
-            halo_copy_2(d).wait_send()
+            for step in range(SUBSTEPS):
+                halo_copy(step, d).wait_send()
             face_copy(d).wait_send()
-            face_copy(d ^ 1).wait_recv()
-
-    loads[10].wait()
-    sweep(pressure_ref, source_ref, face_x_ref, face_y_ref, face_z_ref, result_ref)
-    stores[5].start()
-    for d in range(6):
-
-        @pl.when(there[d][1])
-        def _():
             moved_copy(d).wait_send()
             moved_copy(d ^ 1).wait_recv()
 
@@ -619,7 +617,9 @@
         ]
         for i in range(3):
             force_ref[(i,) + block] = parts[i]
-        result_ref[block] = volume_coeff * parts[3] + drag_weight * parts[2]
+        result_ref[block] = (
+            result_ref[block] + volume_coeff * parts[3] + drag_weight * parts[2]
+        ) / 6.0
 
 
 def sweep(pressure_ref, source_ref, face_x_ref, face_y_ref, face_z_ref, result_ref):
@@ -644,7 +644,7 @@
             jnp.broadcast_to(face_z_ref[1][:, x : x + 1], here.shape),
             pltpu.roll(here, cells_z - 1, 1),
         )
-        result_ref[x] = (total + source_ref[x] + result_ref[x]) / 6.0
+        result_ref[x] = total + source_ref[x]
 
 
 def finish(*refs):
@@ -685,7 +685,6 @@
 ):
     cells_x, cells_y, cells_z = pressure.shape
     f32 = jnp.float32
-    smem = pl.BlockSpec(memory_space=pltpu.SMEM)
     far = pl.BlockSpec(memory_space=pltpu.HBM)
     shape = jax.ShapeDtypeStruct
     rows = (BINS, SLOTS)
@@ -702,12 +701,13 @@
     made = pl.pallas_call(
         particles,
         out_shape=results,
-        in_specs=[smem] + [far] * 11,
+        in_specs=[far] * 12,
         out_specs=(far,) * 8,
         scratch_shapes=[
             pltpu.VMEM((9,) + rows, f32),
             pltpu.VMEM((3 * HIST,) + rows, f32),
             pltpu.VMEM((3,) + rows, f32),
+            pltpu.SMEM(counts.shape, jnp.int32),
             pltpu.VMEM((3,) + rows, f32),
             pltpu.VMEM((3,) + rows, f32),
             pltpu.VMEM((3,) + rows, f32),
@@ -727,10 +727,10 @@
             pltpu.VMEM((7, 3) + rows, f32),
             pltpu.VMEM((7, BINS, SLOTS, SLOTS), f32),
             pltpu.VMEM((3, BINS, SLOTS, SLOTS), f32),
-            pltpu.VMEM((10,) + rows, f32),
-            pltpu.VMEM((6, 10) + rows, f32),
             pltpu.VMEM((9,) + rows, f32),
-            pltpu.VMEM((6, 9) + rows, f32),
+            pltpu.VMEM((9,) + rows, f32),
+            pltpu.VMEM((SUBSTEPS, 6, 5) + rows, f32),
+            pltpu.VMEM((SUBSTEPS, 6, 5) + rows, f32),
             pltpu.VMEM((BINS, 32, SLOTS), f32),
             pltpu.VMEM((6, 32, SLOTS), f32),
             pltpu.VMEM((6, 32, SLOTS), f32),
@@ -739,7 +739,7 @@
             pltpu.VMEM((2, cells_y, cells_z), f32),
             pltpu.VMEM((2, cells_x, cells_z), f32),
             pltpu.VMEM((2, cells_y, SLOTS), f32),
-            pltpu.SemaphoreType.DMA((11,)),
+            pltpu.SemaphoreType.DMA((12,)),
             pltpu.SemaphoreType.DMA((9,)),
             pltpu.SemaphoreType.DMA((4, 6)),
             pltpu.SemaphoreType.DMA((4, 6)),

time: 27 us -> 25.6 us (0.948)
  Pallas kernels: 26.2 us -> 24.8 us
    pallas_call x1, Pallas kernels: 23.6 us -> 22.3 us  [body(): pl.pallas_call(particles, out_shape=results, in_specs=[far] * 12, out_spe...]
where the time goes in v4:
time: 25.6 us; the launch traced here: 25.5 us
  Pallas kernels  24.8 us (97%)
  between operations  0.65 us (3%)
    pallas_call x1, Pallas kernels, body(): pl.pallas_call(particles, out_shape=results, in_specs=[far] * 12, out_spe...  22.3 us
    pallas_call x1, Pallas kernels, body(): pl.pallas_call(finish, out_shape=results, in_specs=[far] * 8, out_specs=(...  2.56 us

profile of v4, /device:TPU:1, one launch (start us, length us, event | category | flops | bytes accessed | tf_op | source)
XLA Modules:
  0.0 25.5 jit_solution(11429487297361503346)
XLA Ops:
  0.6 22.3 %shard_map.179 = (f32[3,8,128]{2,1,0:T(8,128)}, f32[3,8,128]{2,1,0:T(8,128)}, f32[3,8,128]{2,1,0:T(8,128)}, f32[12,8,128]{2,1,0:T(8,128)}, f32[3,16,32,256]{3,2,...) custom-call(s32[2,2,2]{2,1,0:T(2,128)} %counts_hbm.1, f32[3,8,128]{2,1,0:T(8,128)} %bitcast.20, ...), custom_call_target="tpu_custom_call" | custom-call | tf_op jit(solution)/shard_map/pallas_call | solution.py:701
  22.9 2.6 %shard_map.180 = (f32[3,8,128]{2,1,0:T(8,128)}, f32[3,8,128]{2,1,0:T(8,128)}, f32[3,8,128]{2,1,0:T(8,128)}, f32[12,8,128]{2,1,0:T(8,128)}, f32[3,16,32,256]{3,2,...) custom-call(f32[3,8,128]{2,1,0:T(8,128)} %get-tuple-element.24.refs_0_, ...), custom_call_target="tpu_custom_call" | custom-call | tf_op jit(solution)/shard_map/pallas_call | solution.py:764

commit v5 on v4

--- a/solution.py
+++ b/solution.py
@@ -136,9 +136,9 @@
         bin_pairs(mine_ref, table_ref, scaled_ref, (0, 1, 2, 3), sums_ref, True, b)
 
 
-def outer_pairs(mine_ref, table_ref, scaled_ref, sums_ref):
+def outer_pairs(mine_ref, table_ref, scaled_ref, tables, sums_ref):
     def one(b, carry):
-        bin_pairs(mine_ref, table_ref, scaled_ref, (4, 5, 6), sums_ref, False, b)
+        bin_pairs(mine_ref, table_ref, scaled_ref, tables, sums_ref, False, b)
         return carry
 
     lax.fori_loop(0, BINS, one, 0)
@@ -370,8 +370,8 @@
             for i in range(3):
                 scaled_ref[t, i] = table_ref[t, 3 + i] * SPEED_SCALE
 
-    def outer_tables(step):
-        for axis in range(3):
+    def outer_tables(step, axes):
+        for axis in axes:
             for n in range(5):
                 low, high = halo_ref[step, 2 * axis, n], halo_ref[step, 2 * axis + 1, n]
                 first = jnp.where(bits[axis] == 0, swapped(low, axis), swapped(high, axis))
@@ -448,14 +448,15 @@
             loads[11].wait()
             sweep(pressure_ref, source_ref, face_x_ref, face_y_ref, face_z_ref, result_ref)
 
-        for d in range(6):
-
-            @pl.when(there[d][1])
-            def _():
-                halo_copy(step, d ^ 1).wait_recv()
-
-        outer_tables(step)
-        outer_pairs(mine_ref, table_ref, scaled_ref, sums_ref)
+        for axes in ((1, 2), (0,)):
+            for d in [2 * axis + side for axis in axes for side in range(2)]:
+
+                @pl.when(there[d][1])
+                def _():
+                    halo_copy(step, d ^ 1).wait_recv()
+
+            outer_tables(step, axes)
+            outer_pairs(mine_ref, table_ref, scaled_ref, [4 + axis for axis in axes], sums_ref)
         normal = [lane_sums(sums_ref, i) for i in range(3)]
 
         places, speeds, turning = fields[0:3], fields[3:6], fields[6:9]

time: 25.6 us -> 25.9 us (1.012)
  Pallas kernels: 24.8 us -> 25.1 us
    pallas_call x1, Pallas kernels: 22.3 us -> 22.5 us  [body(): pl.pallas_call(particles, out_shape=results, in_specs=[far] * 12, out_spe...]
where the time goes in v5:
time: 25.9 us; the launch traced here: 25.8 us
  Pallas kernels  25.1 us (97%)
  between operations  0.65 us (3%)
    pallas_call x1, Pallas kernels, body(): pl.pallas_call(particles, out_shape=results, in_specs=[far] * 12, out_spe...  22.5 us
    pallas_call x1, Pallas kernels, body(): pl.pallas_call(finish, out_shape=results, in_specs=[far] * 8, out_specs=(...  2.56 us

profile of v5, /device:TPU:1, one launch (start us, length us, event | category | flops | bytes accessed | tf_op | source)
XLA Modules:
  0.0 25.8 jit_solution(1735009592674202612)
XLA Ops:
  0.6 22.5 %shard_map.179 = (f32[3,8,128]{2,1,0:T(8,128)}, f32[3,8,128]{2,1,0:T(8,128)}, f32[3,8,128]{2,1,0:T(8,128)}, f32[12,8,128]{2,1,0:T(8,128)}, f32[3,16,32,256]{3,2,...) custom-call(s32[2,2,2]{2,1,0:T(2,128)} %counts_hbm.1, f32[3,8,128]{2,1,0:T(8,128)} %bitcast.20, ...), custom_call_target="tpu_custom_call" | custom-call | tf_op jit(solution)/shard_map/pallas_call | solution.py:702
  23.2 2.6 %shard_map.180 = (f32[3,8,128]{2,1,0:T(8,128)}, f32[3,8,128]{2,1,0:T(8,128)}, f32[3,8,128]{2,1,0:T(8,128)}, f32[12,8,128]{2,1,0:T(8,128)}, f32[3,16,32,256]{3,2,...) custom-call(f32[3,8,128]{2,1,0:T(8,128)} %get-tuple-element.24.refs_0_, ...), custom_call_target="tpu_custom_call" | custom-call | tf_op jit(solution)/shard_map/pallas_call | solution.py:765

commit v6 on v4

--- a/solution.py
+++ b/solution.py
@@ -310,54 +310,6 @@
         own_ref[6 + i] = spin_ref[i]
     bits = bin_bits()
 
-    def send_halo(step, fields):
-        for d in range(6):
-            axis = d // 2
-            for n in range(5):
-                packed_ref[step, d, n] = jnp.where(
-                    bits[axis] == d % 2, fields[2 * n], swapped(fields[2 * n + 1], axis)
-                )
-        if step == 0:
-            pl.semaphore_wait(barrier, sum(there[d][1].astype(jnp.int32) for d in range(6)))
-        for d in range(6):
-
-            @pl.when(there[d][1])
-            def _():
-                halo_copy(step, d).start()
-
-
-    for s in range(6):
-
-        @pl.when(jnp.logical_not(there[s][1]))
-        def _():
-            for step in range(SUBSTEPS):
-                halo_ref[step, s] = jnp.zeros((5, BINS, SLOTS), jnp.float32)
-                halo_ref[step, s, 4] = jnp.full((BINS, SLOTS), NOBODY, jnp.float32)
-            come_ref[s ^ 1] = jnp.zeros((32, SLOTS), jnp.float32)
-            face = (face_x_ref, face_y_ref, face_z_ref)[s // 2]
-            face[s % 2] = jnp.zeros(face.shape[1:], jnp.float32)
-
-    send_halo(0, [own_ref[f] for f in range(9)] + [partner_radius])
-    for load in loads[5:10]:
-        load.wait()
-    code = [partners_ref[k] for k in range(HIST)]
-    valid = [jnp.where(code[k] >= 0, 1.0, 0.0) for k in range(HIST)]
-    member = [jnp.maximum(code[k], 0) & (SLOTS - 1) for k in range(HIST)]
-    which = [lax.shift_right_logical(jnp.maximum(code[k], 0), 7) for k in range(HIST)]
-
-    def masks_of(k):
-        found = [which[k] == 0]
-        for axis in range(3):
-            found.append(which[k] == 2 * axis + 2 - bits[axis])
-        for axis in range(3):
-            found.append(which[k] == 2 * axis + 1 + bits[axis])
-        return found
-
-    safe = jnp.where(radius > 0.0, radius, 1.0)
-    mass = safe * 10.0
-    mass = mass * mass * mass
-    inertia = 0.4 * mass * safe * safe
-
     def inner_tables(fields):
         for f in range(10):
             table_ref[0, f] = fields[f]
@@ -369,6 +321,55 @@
         for t in range(4):
             for i in range(3):
                 scaled_ref[t, i] = table_ref[t, 3 + i] * SPEED_SCALE
+
+    def send_halo(step, fields):
+        for d in range(6):
+            axis = d // 2
+            for n in range(5):
+                packed_ref[step, d, n] = jnp.where(
+                    bits[axis] == d % 2, fields[2 * n], swapped(fields[2 * n + 1], axis)
+                )
+        if step == 0:
+            inner_tables(fields)
+            pl.semaphore_wait(barrier, sum(there[d][1].astype(jnp.int32) for d in range(6)))
+        for d in range(6):
+
+            @pl.when(there[d][1])
+            def _():
+                halo_copy(step, d).start()
+
+
+    for s in range(6):
+
+        @pl.when(jnp.logical_not(there[s][1]))
+        def _():
+            for step in range(SUBSTEPS):
+                halo_ref[step, s] = jnp.zeros((5, BINS, SLOTS), jnp.float32)
+                halo_ref[step, s, 4] = jnp.full((BINS, SLOTS), NOBODY, jnp.float32)
+            come_ref[s ^ 1] = jnp.zeros((32, SLOTS), jnp.float32)
+            face = (face_x_ref, face_y_ref, face_z_ref)[s // 2]
+            face[s % 2] = jnp.zeros(face.shape[1:], jnp.float32)
+
+    send_halo(0, [own_ref[f] for f in range(9)] + [partner_radius])
+    for load in loads[5:10]:
+        load.wait()
+    code = [partners_ref[k] for k in range(HIST)]
+    valid = [jnp.where(code[k] >= 0, 1.0, 0.0) for k in range(HIST)]
+    member = [jnp.maximum(code[k], 0) & (SLOTS - 1) for k in range(HIST)]
+    which = [lax.shift_right_logical(jnp.maximum(code[k], 0), 7) for k in range(HIST)]
+
+    def masks_of(k):
+        found = [which[k] == 0]
+        for axis in range(3):
+            found.append(which[k] == 2 * axis + 2 - bits[axis])
+        for axis in range(3):
+            found.append(which[k] == 2 * axis + 1 + bits[axis])
+        return found
+
+    safe = jnp.where(radius > 0.0, radius, 1.0)
+    mass = safe * 10.0
+    mass = mass * mass * mass
+    inertia = 0.4 * mass * safe * safe
 
     def outer_tables(step):
         for axis in range(3):
@@ -407,7 +408,8 @@
     for step in range(SUBSTEPS):
         source = own_ref if step == 0 else own_2_ref
         fields = [source[f] for f in range(9)] + [partner_radius]
-        inner_tables(fields)
+        if step > 0:
+            inner_tables(fields)
         inner_pairs(radii_ref, mine_ref, table_ref, scaled_ref, sums_ref)
 
         if step == 0:
@@ -437,16 +439,6 @@
                         axis=0,
                         keepdims=True,
                     )
-
-        if step == 1:
-            for d in range(6):
-
-                @pl.when(there[d][1])
-                def _():
-                    face_copy(d ^ 1).wait_recv()
-
-            loads[11].wait()
-            sweep(pressure_ref, source_ref, face_x_ref, face_y_ref, face_z_ref, result_ref)
 
         for d in range(6):
 
@@ -557,6 +549,14 @@
 
     deposit(counts_ref, radii_ref, cells_ref, state_out, gas_out, force_ref, result_ref)
     stores[4].start()
+    for d in range(6):
+
+        @pl.when(there[d][1])
+        def _():
+            face_copy(d ^ 1).wait_recv()
+
+    loads[11].wait()
+    sweep(pressure_ref, source_ref, face_x_ref, face_y_ref, face_z_ref, result_ref)
     stores[5].start()
     for d in range(6):
 
@@ -617,9 +617,7 @@
         ]
         for i in range(3):
             force_ref[(i,) + block] = parts[i]
-        result_ref[block] = (
-            result_ref[block] + volume_coeff * parts[3] + drag_weight * parts[2]
-        ) / 6.0
+        result_ref[block] = volume_coeff * parts[3] + drag_weight * parts[2]
 
 
 def sweep(pressure_ref, source_ref, face_x_ref, face_y_ref, face_z_ref, result_ref):
@@ -644,7 +642,7 @@
             jnp.broadcast_to(face_z_ref[1][:, x : x + 1], here.shape),
             pltpu.roll(here, cells_z - 1, 1),
         )
-        result_ref[x] = total + source_ref[x]
+        result_ref[x] = (total + source_ref[x] + result_ref[x]) / 6.0
 
 
 def finish(*refs):

time: 25.6 us -> 25.6 us (level)
  no operation moved by 1% of the time
where the time goes in v6:
time: 25.6 us; the launch traced here: 25.5 us
  Pallas kernels  24.8 us (97%)
  between operations  0.65 us (3%)
    pallas_call x1, Pallas kernels, body(): pl.pallas_call(particles, out_shape=results, in_specs=[far] * 12, out_spe...  22.3 us
    pallas_call x1, Pallas kernels, body(): pl.pallas_call(finish, out_shape=results, in_specs=[far] * 8, out_specs=(...  2.56 us

profile of v6, /device:TPU:1, one launch (start us, length us, event | category | flops | bytes accessed | tf_op | source)
XLA Modules:
  0.0 25.5 jit_solution(11763366843619555753)
XLA Ops:
  0.6 22.3 %shard_map.179 = (f32[3,8,128]{2,1,0:T(8,128)}, f32[3,8,128]{2,1,0:T(8,128)}, f32[3,8,128]{2,1,0:T(8,128)}, f32[12,8,128]{2,1,0:T(8,128)}, f32[3,16,32,256]{3,2,...) custom-call(s32[2,2,2]{2,1,0:T(2,128)} %counts_hbm.1, f32[3,8,128]{2,1,0:T(8,128)} %bitcast.20, ...), custom_call_target="tpu_custom_call" | custom-call | tf_op jit(solution)/shard_map/pallas_call | solution.py:699
  22.9 2.6 %shard_map.180 = (f32[3,8,128]{2,1,0:T(8,128)}, f32[3,8,128]{2,1,0:T(8,128)}, f32[3,8,128]{2,1,0:T(8,128)}, f32[12,8,128]{2,1,0:T(8,128)}, f32[3,16,32,256]{3,2,...) custom-call(f32[3,8,128]{2,1,0:T(8,128)} %get-tuple-element.24.refs_0_, ...), custom_call_target="tpu_custom_call" | custom-call | tf_op jit(solution)/shard_map/pallas_call | solution.py:762
